TPU v7x, 256 devices: a whole 4x4x8 slice. The times are simulated.
256 devices in a mesh: row: 32 (over x, z_hi, core), walk: 8 (over y, z_lo).
Axes of the slice: x: 4, y: 4, z: 8 (z_hi: 4, z_lo: 2; z = z_hi * 2 + z_lo), core: 2. Of those that a mesh axis runs over, the one named last changes fastest.
Arguments:
- cholesky: bfloat16 [256, 1024, 1024], P(None, 'row'), may hold values from -0.125 to 0.125
- walkers: bfloat16 [256, 1024, 256], P('walk', 'row'), may hold values from -6 to 6
- trial_orbitals: bfloat16 [1024, 256], P('row'), may hold values from -0.015625 to 0.015625
- fields: float32 [2, 256, 256], P(None, 'walk'), may hold values from -6 to 6
- log_weights: float32 [256], P('walk'), may hold values from -1.2 to 2.4
Outputs:
- walkers_out: bfloat16 [256, 1024, 256], P('walk', 'row')
- log_weights_out: float32 [256], P('walk')
All inputs are finite; a program needn't handle non-finite values.
Results may differ from a plain program's by a relative error of at most 0.025.
Values may be sent and summed in bfloat16 or wider, within the bound.
No kernel may reach another device: no remote copies, remote signals or barrier semaphores. Data moves between devices by JAX's collectives and lax.ppermute only.
A program may use at most 128 MiB of HBM per device.

v0:
```python
import functools

import jax
import jax.numpy as jnp
from jax import lax
from jax.experimental import pallas as pl
from jax.experimental.pallas import tpu as pltpu
from jax.sharding import Mesh, PartitionSpec as P

ROW = ("x", "zh", "c")
WALK = ("y", "zl")

block_rows = 8
time_root = 0.1
WHOLE = pl.BlockSpec(memory_space=pltpu.VMEM)
IN_HBM = pl.BlockSpec(memory_space=pltpu.HBM)
LAST = (((1,), (1,)), ((), ()))


def params(mebibytes):
    return pltpu.CompilerParams(vmem_limit_bytes=mebibytes * 2**20)


def cost(flops, size):
    return pl.CostEstimate(flops=flops, bytes_accessed=size, transcendentals=0)


def dot(left, right, dims=(((1,), (0,)), ((), ())), precision=None):
    return lax.dot_general(left, right, dims, precision=precision, preferred_element_type=jnp.float32)


def diagonal(walkers):
    shape = (1, block_rows, walkers * block_rows)
    lane = lax.broadcasted_iota(jnp.int32, shape, 2) % block_rows
    return lane == lax.broadcasted_iota(jnp.int32, shape, 1)


def reduce_diagonal(cross, walkers):
    kept = jnp.sum(jnp.where(diagonal(walkers), cross, 0.0), axis=1)
    shape = (walkers, walkers * block_rows)
    lane = lax.broadcasted_iota(jnp.int32, shape, 1) // block_rows
    pick = (lane == lax.broadcasted_iota(jnp.int32, shape, 0)).astype(jnp.float32)
    return dot(pick, kept, LAST, precision=lax.Precision.HIGHEST)


def diagonal(walkers):
    shape = (1, block_rows, walkers * block_rows)
    lane = lax.broadcasted_iota(jnp.int32, shape, 2) % block_rows
    return lane == lax.broadcasted_iota(jnp.int32, shape, 1)


def reduce_diagonal(cross, walkers):
    kept = jnp.sum(jnp.where(diagonal(walkers), cross, 0.0), axis=1)
    shape = (walkers, walkers * block_rows)
    lane = lax.broadcasted_iota(jnp.int32, shape, 1) // block_rows
    pick = (lane == lax.broadcasted_iota(jnp.int32, shape, 0)).astype(jnp.float32)
    return dot(pick, kept, LAST, precision=lax.Precision.HIGHEST)


def in_vmem(value):
    return pltpu.with_memory_space_constraint(value, pltpu.VMEM)


def pieces(vectors, rows):
    some = 512 // block_rows
    return [
        (slice(low, low + some), slice(start, start + block_rows))
        for low in range(0, vectors, some)
        for start in range(0, rows, block_rows)
    ]


def add_diagonal(rotated, phi_ref, at, some, cross_ref):
    right = phi_ref[:, at, :].reshape(-1, phi_ref.shape[2])
    cross = dot(rotated, right, LAST).reshape(-1, block_rows, right.shape[0])
    if at.start:
        cross = cross + cross_ref[some]
    cross_ref[some] = cross


def bias_kernel(rotated_ref, phi_ref, part_ref, cross_ref):
    vectors, rows, electrons = rotated_ref.shape
    for some, at in pieces(vectors, rows):
        add_diagonal(rotated_ref[some, at, :].reshape(-1, electrons), phi_ref, at, some, cross_ref)
    part_ref[...] = reduce_diagonal(cross_ref[...], phi_ref.shape[0])


def bias(rotated, phi):
    vectors = rotated.shape[0]
    walkers = phi.shape[0]
    return pl.pallas_call(
        bias_kernel,
        in_specs=[WHOLE] * 2,
        out_specs=WHOLE,
        out_shape=jax.ShapeDtypeStruct((walkers, vectors), jnp.float32),
        scratch_shapes=[pltpu.VMEM((vectors, block_rows, walkers * block_rows), jnp.float32)],
        compiler_params=params(12),
        cost_estimate=cost(2**30, 2**22),
    )(rotated, phi)


def fetch(chol_hbm, chol_ref, arrived):
    vectors, rows, _ = chol_ref.shape
    half = vectors // 2
    copies = {}
    for start in range(0, rows, block_rows):
        for low in range(0, vectors, half):
            at = (slice(low, low + half), slice(start, start + block_rows))
            copy = pltpu.make_async_copy(chol_hbm.at[at], chol_ref.at[at], arrived.at[len(copies)])
            copy.start()
            copies[start, low] = copy
    return copies


def first_bias_kernel(chol_hbm, trial_ref, phi_ref, part_ref, chol_ref, paired_ref, cross_ref, arrived):
    vectors, rows, orbitals = chol_ref.shape
    incoming = fetch(chol_hbm, chol_ref, arrived)
    for start in range(0, rows, block_rows):
        phi = phi_ref[:, start : start + block_rows, :].reshape(-1, phi_ref.shape[2])
        paired_ref[start // block_rows] = dot(phi, trial_ref[...], LAST).astype(jnp.bfloat16)
    some = 512 // block_rows
    for start in range(0, rows, block_rows):
        for low in range(0, vectors, some):
            if (start, low) in incoming:
                incoming[start, low].wait()
            piece = chol_ref[low : low + some, start : start + block_rows, :].reshape(-1, orbitals)
            cross = dot(piece, paired_ref[start // block_rows], LAST).reshape(some, block_rows, -1)
            if start:
                cross = cross + cross_ref[low : low + some]
            cross_ref[low : low + some] = cross
    part_ref[...] = reduce_diagonal(cross_ref[...], phi_ref.shape[0])


def first_bias(chol, trial, phi):
    vectors, rows, orbitals = chol.shape
    walkers = phi.shape[0]
    blocks = rows // block_rows
    wide = walkers * block_rows
    return pl.pallas_call(
        first_bias_kernel,
        in_specs=[IN_HBM, WHOLE, WHOLE],
        out_specs=WHOLE,
        out_shape=jax.ShapeDtypeStruct((walkers, vectors), jnp.float32),
        scratch_shapes=[
            pltpu.VMEM(chol.shape, chol.dtype),
            pltpu.VMEM((blocks, wide, orbitals), jnp.bfloat16),
            pltpu.VMEM((vectors, block_rows, wide), jnp.float32),
            pltpu.SemaphoreType.DMA((2 * blocks,)),
        ],
        compiler_params=params(50),
        cost_estimate=cost(2**32, 2**24),
    )(chol, trial, phi)


def rotate_kernel(chol_hbm, trial_ref, rotated_hbm, chol_ref, rotated_ref, arrived, left):
    vectors, rows, orbitals = chol_ref.shape
    electrons = trial_ref.shape[1]
    incoming = fetch(chol_hbm, chol_ref, arrived)
    outgoing = []
    for start in range(0, rows, block_rows):
        at = slice(start, start + block_rows)
        for low in range(0, vectors, 512 // block_rows):
            if (start, low) in incoming:
                incoming[start, low].wait()
            some = slice(low, low + 512 // block_rows)
            piece = chol_ref[some, at, :].reshape(-1, orbitals)
            rotated = dot(piece, trial_ref[...]).astype(jnp.bfloat16)
            rotated_ref[some, at, :] = rotated.reshape(-1, block_rows, electrons)
        copy = pltpu.make_async_copy(
            rotated_ref.at[:, at], rotated_hbm.at[:, at], left.at[start // block_rows]
        )
        copy.start()
        outgoing.append(copy)
    for copy in outgoing:
        copy.wait()


def rotate(chol, trial):
    vectors, rows, _ = chol.shape
    blocks = rows // block_rows
    shape = (vectors, rows, trial.shape[1])
    return pl.pallas_call(
        rotate_kernel,
        in_specs=[IN_HBM, WHOLE],
        out_specs=IN_HBM,
        out_shape=jax.ShapeDtypeStruct(shape, jnp.bfloat16),
        scratch_shapes=[
            pltpu.VMEM(chol.shape, chol.dtype),
            pltpu.VMEM(shape, jnp.bfloat16),
            pltpu.SemaphoreType.DMA((2 * blocks,)),
            pltpu.SemaphoreType.DMA((blocks,)),
        ],
        compiler_params=params(50),
        cost_estimate=cost(2**32, 2**24),
    )(chol, trial)


def potential_kernel(mixed_ref, chol_hbm, out_ref, wide_ref, chol_ref, arrived):
    walkers, vectors = mixed_ref.shape
    _, rows, orbitals = chol_ref.shape
    incoming = fetch(chol_hbm, chol_ref, arrived)
    keep = diagonal(256 // block_rows)
    g = lax.broadcasted_iota(jnp.int32, (vectors, 256), 0)
    lane = lax.broadcasted_iota(jnp.int32, (vectors, 256), 1) // block_rows
    for start in range(0, vectors * block_rows, 256):
        pick = (g == start // block_rows + lane).astype(jnp.bfloat16)
        wide = jnp.where(keep, dot(mixed_ref[...], pick)[:, None, :], 0.0)
        wide_ref[:, start : start + 256] = wide.reshape(-1, 256).astype(jnp.bfloat16)
    for start in range(0, rows, block_rows):
        at = slice(start, start + block_rows)
        incoming[start, 0].wait()
        incoming[start, vectors // 2].wait()
        for low in range(0, orbitals, 256):
            right = chol_ref[:, at, low : low + 256].reshape(vectors * block_rows, 256)
            out = time_root * dot(wide_ref[...], right)
            out_ref[:, at, low : low + 256] = out.astype(jnp.bfloat16).reshape(walkers, block_rows, 256)


def potential(mixed, chol):
    walkers, vectors = mixed.shape
    _, rows, orbitals = chol.shape
    return pl.pallas_call(
        potential_kernel,
        in_specs=[WHOLE, IN_HBM],
        out_specs=WHOLE,
        out_shape=jax.ShapeDtypeStruct((walkers, rows, orbitals), jnp.bfloat16),
        scratch_shapes=[
            pltpu.VMEM((walkers * block_rows, vectors * block_rows), jnp.bfloat16),
            pltpu.VMEM(chol.shape, chol.dtype),
            pltpu.SemaphoreType.DMA((2 * rows // block_rows,)),
        ],
        compiler_params=params(50),
    )(mixed, chol)


def exchange(value, axis):
    return lax.all_to_all(value, axis, split_axis=0, concat_axis=0, tiled=True)


def swap(value, axis):
    return lax.ppermute(value, axis, [(0, 1), (1, 0)])


def spread(value, axis):
    count = lax.axis_size(axis)
    return exchange(jnp.broadcast_to(value[None], (count,) + value.shape), axis)


def ring_sum(value, axis):
    total = value
    for shift in range(1, 4):
        total = total + lax.ppermute(value, axis, [(i, (i + shift) % 4) for i in range(4)])
    return total


def row_sum(part, by_permutes):
    core = lax.axis_index("c")
    count = part.shape[0] // 2
    halves = part.reshape((2, count) + part.shape[1:])
    mine = lax.dynamic_index_in_dim(halves, core, 0, False)
    other = lax.dynamic_index_in_dim(halves, 1 - core, 0, False)
    total = mine + swap(other, "c")
    if by_permutes:
        total = ring_sum(ring_sum(total, "x"), "zh")
    else:
        total = jnp.sum(spread(total, ("x", "zh")), axis=0)
    other = swap(total, "c")
    return jnp.where(
        core == 0,
        jnp.concatenate([total, other]),
        jnp.concatenate([other, total]),
    )


def gather_trial(rows):
    core = lax.axis_index("c")
    mine = spread(rows, ("x", "zh"))
    other = swap(mine, "c")
    both = jnp.where(core == 0, jnp.stack([mine, other], 1), jnp.stack([other, mine], 1))
    return both.reshape(-1, rows.shape[-1])


def taylor(potential, walker):
    summed = walker.astype(jnp.float32)
    power_term = walker
    for degree in range(1, 5):
        next_term = jnp.dot(potential, power_term, preferred_element_type=jnp.float32) / degree
        summed = summed + next_term
        power_term = next_term.astype(jnp.bfloat16)
    return summed.astype(jnp.bfloat16)


def shards(cholesky, walkers, trial_orbitals, fields, log_weights):
    vectors, rows, orbitals = cholesky.shape
    walker_count, _, electrons = walkers.shape
    trial = gather_trial(trial_orbitals)
    phi = exchange(walkers, ROW).reshape(orbitals, electrons)
    part = first_bias(cholesky, trial, walkers)
    weights_now = log_weights
    steps = fields.shape[0]
    for step in range(steps):
        shifted = time_root * row_sum(part, by_permutes=step == 0)
        aux_field = fields[step]
        weights_now = weights_now + jnp.sum(aux_field * shifted - 0.5 * shifted * shifted, axis=1)
        mixed = (aux_field - shifted).astype(jnp.bfloat16)
        sent = potential(mixed, cholesky)
        if step == 0:
            sent, trial, phi = lax.optimization_barrier((sent, trial, phi))
            rotated = rotate(cholesky, trial)
        if step == steps - 1:
            pair_sum = jnp.full((8, 128), jnp.sum(jnp.exp(weights_now)))
            pair_sum = pair_sum + swap(pair_sum, "zl")
            sent, pair_sum = lax.optimization_barrier((sent, pair_sum))
        sent = exchange(sent, ROW).reshape(orbitals, orbitals)
        if step == 0:
            sent, rotated = lax.optimization_barrier((sent, rotated))
        if step == steps - 1:
            weight_sum = ring_sum(pair_sum, "y")[0, 0]
            count = walker_count * lax.axis_size(WALK)
            weights_now = weights_now - jnp.log(weight_sum / count)
        phi = taylor(sent, phi)
        if step == steps - 1:
            phi, weights_now = lax.optimization_barrier((phi, weights_now))
        phi_rows = exchange(phi.reshape(walker_count, rows, electrons), ROW)
        if step < steps - 1:
            part = bias(rotated, phi_rows)
    return phi_rows, weights_now


def solution(mesh):
    split = Mesh(mesh.devices.reshape(4, 4, 2, 4, 2), ROW + WALK)
    placed = (
        P(None, ROW, None),
        P(WALK, ROW, None),
        P(ROW, None),
        P(None, WALK, None),
        P(WALK),
    )
    return jax.shard_map(
        shards,
        mesh=split,
        in_specs=placed,
        out_specs=(P(WALK, ROW, None), P(WALK)),
        check_vma=False,
    )
```

profile of v0, /device:TPU:6, one launch (start us, length us, event | category | flops | bytes accessed | tf_op | source)
XLA Modules:
  0.0 268.2 jit_solution(14141525606649377498)
XLA Ops:
  1.4 22.2 %all_to_all.35 = bf16[16,32,256]{2,1,0:T(8,128)(2,1)S(1)} all-to-all(bf16[16,32,256]{2,1,0:T(8,128)(2,1)S(1)} %broadcast_in_dim.6), channel_id=1, replica_groups=mesh['x'=4,'zh'=4,'c'=2,'y'=4,'zl'=2] {'x','zh'}, dimensions={0} | all-to-all | bytes 524288 | tf_op jit(solution)/shard_map/all_to_all | solution.py:237
  23.6 6.1 %all-to-all-start.1 = ((bf16[32,32,256]{2,1,0:T(8,128)(2,1)}), bf16[32,32,256]{2,1,0:T(8,128)(2,1)S(1)}, u32[]{:S(2)}, u32[]{:S(2)}) async-start(bf16[32,32,256]{2,1,0:T(8,128)(2,1)} %phi_ref.1), calls=%async_computation.1 | async-start | bytes 1048576 | tf_op jit(solution)/shard_map/all_to_all | solution.py:237
  29.8 8.4 %shard_map.68 = f32[32,256]{1,0:T(8,128)S(1)} custom-call(bf16[256,32,1024]{2,1,0:T(8,128)(2,1)} %chol_hbm.7, bf16[1024,256]{1,0:T(8,128)(2,1)S(1)} %bitcast.47, bf16[32,32,256]{2,1,0:T(8,128)(2,1)S(1)} %copy-done.1), custom_call_target="tpu_custom_call" | custom-call | flops 4294967296 | bytes 16777216 | tf_op jit(solution)/shard_map/pallas_call | solution.py:139
  41.2 2.3 collective-permute-start.2
  45.7 3.6 %collective-permute-start.7 = (f32[16,256]{1,0:T(8,128)S(1)}, f32[16,256]{1,0:T(8,128)S(1)}, u32[]{:S(2)}, u32[]{:S(2)}) collective-permute-start(f32[16,256]{1,0:T(8,128)S(1)} %add_add_fusion.1), channel_id=1, source_target_pairs={{0,48},{16,0},{32,16},{48,32},{1,49},{17,1},{33,17},{49,33},{2,50}... | collective-permute-start | bytes 49160 | tf_op jit(solution)/shard_map/ppermute | solution.py:252
  49.3 2.3 collective-permute-start.6
  51.6 2.4 collective-permute-start.5
  54.0 2.9 %collective-permute-done.6 = f32[16,256]{1,0:T(8,128)S(1)} collective-permute-done((f32[16,256]{1,0:T(8,128)S(1)}, f32[16,256]{1,0:T(8,128)S(1)}, u32[]{:S(2)}, u32[]{:S(2)}) %collective-permute-start.6) | collective-permute-done | bytes 16416 | tf_op jit(solution)/shard_map/ppermute | solution.py:252
  57.6 1.2 collective-permute-done.8
  58.8 8.8 %shard_map.69 = bf16[32,32,1024]{2,1,0:T(8,128)(2,1)} custom-call(bf16[32,256]{1,0:T(8,128)(2,1)S(1)} %fusion.13.mixed_ref, bf16[256,32,1024]{2,1,0:T(8,128)(2,1)} %chol_hbm.7), custom_call_target="tpu_custom_call" | custom-call | tf_op jit(solution)/shard_map/pallas_call | solution.py:222
  67.7 8.7 %all-to-all-start.2 = ((bf16[32,32,1024]{2,1,0:T(8,128)(2,1)}), bf16[32,32,1024]{2,1,0:T(8,128)(2,1)S(1)}, u32[]{:S(2)}, u32[]{:S(2)}) async-start(bf16[32,32,1024]{2,1,0:T(8,128)(2,1)} %shard_map.69), calls=%async_computation.2 | async-start | bytes 4194304 | tf_op jit(solution)/shard_map/all_to_all | solution.py:237
  76.5 8.6 %shard_map.70.rotated_ref = bf16[256,32,256]{2,1,0:T(8,128)(2,1)} custom-call(bf16[256,32,1024]{2,1,0:T(8,128)(2,1)} %chol_hbm.7, bf16[1024,256]{1,0:T(8,128)(2,1)S(1)} %bitcast.48), custom_call_target="tpu_custom_call" | custom-call | flops 4294967296 | bytes 16777216 | tf_op jit(solution)/shard_map/pallas_call | solution.py:182
  85.1 38.2 %all-to-all-done.2 = bf16[32,32,1024]{2,1,0:T(8,128)(2,1)S(1)} async-done(((bf16[32,32,1024]{2,1,0:T(8,128)(2,1)}), bf16[32,32,1024]{2,1,0:T(8,128)(2,1)S(1)}, u32[]{:S(2)}, u32[]{:S(2)}) %all-to-all-start.2) | async-done | bytes 2097184 | tf_op jit(solution)/shard_map/all_to_all | solution.py:237
  126.6 23.4 %all_to_all.36.phi_ref = bf16[32,32,256]{2,1,0:T(8,128)(2,1)S(1)} all-to-all(bf16[32,32,256]{2,1,0:T(8,128)(2,1)S(1)} %bitcast.61), channel_id=1, replica_groups=mesh['x'=4,'zh'=4,'c'=2,'y'=4,'zl'=2] {'x','zh','c'}, dimensions={0} | all-to-all | bytes 1048576 | tf_op jit(solution)/shard_map/all_to_all | solution.py:237
  150.1 1.9 shard_map.71
  152.0 2.3 collective-permute-start.9
  155.2 16.7 %all_to_all.37 = f32[16,16,256]{2,1,0:T(8,128)S(1)} all-to-all(f32[16,16,256]{2,1,0:T(8,128)S(1)} %broadcast_in_dim.7), channel_id=1, replica_groups=mesh['x'=4,'zh'=4,'c'=2,'y'=4,'zl'=2] {'x','zh'}, dimensions={0} | all-to-all | bytes 524288 | tf_op jit(solution)/shard_map/all_to_all | solution.py:237
  172.1 1.2 collective-permute-done.10
  175.7 8.8 %shard_map.72 = bf16[32,32,1024]{2,1,0:T(8,128)(2,1)} custom-call(bf16[32,256]{1,0:T(8,128)(2,1)S(1)} %get-tuple-element.22.mixed_ref, bf16[256,32,1024]{2,1,0:T(8,128)(2,1)} %chol_hbm.7), custom_call_target="tpu_custom_call" | custom-call | tf_op jit(solution)/shard_map/pallas_call | solution.py:222
  185.2 6.2 %all-to-all-start.5 = ((bf16[32,32,1024]{2,1,0:T(8,128)(2,1)}), bf16[32,32,1024]{2,1,0:T(8,128)(2,1)S(1)}, u32[]{:S(2)}, u32[]{:S(2)}) async-start(bf16[32,32,1024]{2,1,0:T(8,128)(2,1)} %shard_map.72), calls=%async_computation.5 | async-start | bytes 4194304 | tf_op jit(solution)/shard_map/all_to_all | solution.py:237
  191.5 3.1 %collective-permute-start.14 = (f32[8,128]{1,0:T(8,128)S(1)}, f32[8,128]{1,0:T(8,128)S(1)}, u32[]{:S(2)}, u32[]{:S(2)}) collective-permute-start(f32[8,128]{1,0:T(8,128)S(1)} %broadcast_add_fusion), channel_id=1, source_target_pairs={{0,6},{2,0},{4,2},{6,4},{1,7},{3,1},{5,3},{7,5},{8,14},{10,8},{12,... | collective-permute-start | bytes 12296 | tf_op jit(solution)/shard_map/ppermute | solution.py:252
  196.1 3.5 %collective-permute-done.13 = f32[8,128]{1,0:T(8,128)S(1)} collective-permute-done((f32[8,128]{1,0:T(8,128)S(1)}, f32[8,128]{1,0:T(8,128)S(1)}, u32[]{:S(2)}, u32[]{:S(2)}) %collective-permute-start.13) | collective-permute-done | bytes 4128 | tf_op jit(solution)/shard_map/ppermute | solution.py:252
  201.7 38.9 %all-to-all-done.5 = bf16[32,32,1024]{2,1,0:T(8,128)(2,1)S(1)} async-done(((bf16[32,32,1024]{2,1,0:T(8,128)(2,1)}), bf16[32,32,1024]{2,1,0:T(8,128)(2,1)S(1)}, u32[]{:S(2)}, u32[]{:S(2)}) %all-to-all-start.5) | async-done | bytes 2097184 | tf_op jit(solution)/shard_map/all_to_all | solution.py:237
  243.6 23.8 %all_to_all.38 = bf16[32,32,256]{2,1,0:T(8,128)(2,1)S(1)} all-to-all(bf16[32,32,256]{2,1,0:T(8,128)(2,1)S(1)} %bitcast.64), channel_id=1, replica_groups=mesh['x'=4,'zh'=4,'c'=2,'y'=4,'zl'=2] {'x','zh','c'}, dimensions={0} | all-to-all | bytes 1048576 | tf_op jit(solution)/shard_map/all_to_all | solution.py:237
  (60 shorter events, 20.9 us)
Async XLA Ops:
  0.6 29.2 %copy-start.1 = (bf16[32,32,256]{2,1,0:T(8,128)(2,1)S(1)}, bf16[32,32,256]{2,1,0:T(8,128)(2,1)}, u32[]{:S(2)}) copy-start(bf16[32,32,256]{2,1,0:T(8,128)(2,1)} %phi_ref.1) | copy-start | bytes 1572868
  23.6 6.1 %collective-permute-start = (bf16[16,32,256]{2,1,0:T(8,128)(2,1)S(1)}, bf16[16,32,256]{2,1,0:T(8,128)(2,1)S(1)}, u32[]{:S(2)}, u32[]{:S(2)}) collective-permute-start(bf16[16,32,256]{2,1,0:T(8,128)(2,1)S(1)} %all_to_all.35), channel_id=1, source_target_pairs={{0,8},{8,0},{1,9},{9,1},{2,10},{10,2},{3,11},{11,3},{4,12},{12,4},... | collective-permute-start | bytes 786440 | tf_op jit(solution)/shard_map/ppermute | solution.py:241
  23.6 44.0 %all-to-all-start.1 = ((bf16[32,32,256]{2,1,0:T(8,128)(2,1)}), bf16[32,32,256]{2,1,0:T(8,128)(2,1)S(1)}, u32[]{:S(2)}, u32[]{:S(2)}) async-start(bf16[32,32,256]{2,1,0:T(8,128)(2,1)} %phi_ref.1), calls=%async_computation.1 | async-start | bytes 1048576 | tf_op jit(solution)/shard_map/all_to_all | solution.py:237
  29.8 29.0 %copy-start.4 = (f32[2,32,256]{2,1,0:T(8,128)S(1)}, f32[2,32,256]{2,1,0:T(8,128)}, u32[]{:S(2)}) copy-start(f32[2,32,256]{2,1,0:T(8,128)} %param.8) | copy-start | bytes 196612
  38.2 1.3 collective-permute-start.1
  39.5 5.1 %collective-permute-start.4 = (f32[16,256]{1,0:T(8,128)S(1)}, f32[16,256]{1,0:T(8,128)S(1)}, u32[]{:S(2)}, u32[]{:S(2)}) collective-permute-start(f32[16,256]{1,0:T(8,128)S(1)} %bitcast_add_fusion.1), channel_id=1, source_target_pairs={{0,192},{64,0},{128,64},{192,128},{1,193},{65,1},{129,65},{193,129... | collective-permute-start | bytes 49160 | tf_op jit(solution)/shard_map/ppermute | solution.py:252
  40.3 5.4 %collective-permute-start.3 = (f32[16,256]{1,0:T(8,128)S(1)}, f32[16,256]{1,0:T(8,128)S(1)}, u32[]{:S(2)}, u32[]{:S(2)}) collective-permute-start(f32[16,256]{1,0:T(8,128)S(1)} %bitcast_add_fusion.1), channel_id=1, source_target_pairs={{0,128},{64,192},{128,0},{192,64},{1,129},{65,193},{129,1},{193,65... | collective-permute-start | bytes 49160 | tf_op jit(solution)/shard_map/ppermute | solution.py:252
  41.2 4.5 %collective-permute-start.2 = (f32[16,256]{1,0:T(8,128)S(1)}, f32[16,256]{1,0:T(8,128)S(1)}, u32[]{:S(2)}, u32[]{:S(2)}) collective-permute-start(f32[16,256]{1,0:T(8,128)S(1)} %bitcast_add_fusion.1), channel_id=1, source_target_pairs={{0,64},{64,128},{128,192},{192,0},{1,65},{65,129},{129,193},{193,1... | collective-permute-start | bytes 49160 | tf_op jit(solution)/shard_map/ppermute | solution.py:252
  45.7 8.3 %collective-permute-start.7 = (f32[16,256]{1,0:T(8,128)S(1)}, f32[16,256]{1,0:T(8,128)S(1)}, u32[]{:S(2)}, u32[]{:S(2)}) collective-permute-start(f32[16,256]{1,0:T(8,128)S(1)} %add_add_fusion.1), channel_id=1, source_target_pairs={{0,48},{16,0},{32,16},{48,32},{1,49},{17,1},{33,17},{49,33},{2,50}... | collective-permute-start | bytes 49160 | tf_op jit(solution)/shard_map/ppermute | solution.py:252
  49.3 7.6 %collective-permute-start.6 = (f32[16,256]{1,0:T(8,128)S(1)}, f32[16,256]{1,0:T(8,128)S(1)}, u32[]{:S(2)}, u32[]{:S(2)}) collective-permute-start(f32[16,256]{1,0:T(8,128)S(1)} %add_add_fusion.1), channel_id=1, source_target_pairs={{0,32},{16,48},{32,0},{48,16},{1,33},{17,49},{33,1},{49,17},{2,34}... | collective-permute-start | bytes 49160 | tf_op jit(solution)/shard_map/ppermute | solution.py:252
  51.6 5.9 %collective-permute-start.5 = (f32[16,256]{1,0:T(8,128)S(1)}, f32[16,256]{1,0:T(8,128)S(1)}, u32[]{:S(2)}, u32[]{:S(2)}) collective-permute-start(f32[16,256]{1,0:T(8,128)S(1)} %add_add_fusion.1), channel_id=1, source_target_pairs={{0,16},{16,32},{32,48},{48,0},{1,17},{17,33},{33,49},{49,1},{2,18}... | collective-permute-start | bytes 49160 | tf_op jit(solution)/shard_map/ppermute | solution.py:252
  57.5 1.3 collective-permute-start.8
  67.7 55.6 %copy-start.2 = (bf16[32,32,256]{2,1,0:T(8,128)(2,1)}, bf16[32,32,256]{2,1,0:T(8,128)(2,1)S(1)}, u32[]{:S(2)}) copy-start(bf16[32,32,256]{2,1,0:T(8,128)(2,1)S(1)} %all-to-all-done.1) | copy-start | bytes 1572868
  67.7 55.6 %all-to-all-start.2 = ((bf16[32,32,1024]{2,1,0:T(8,128)(2,1)}), bf16[32,32,1024]{2,1,0:T(8,128)(2,1)S(1)}, u32[]{:S(2)}, u32[]{:S(2)}) async-start(bf16[32,32,1024]{2,1,0:T(8,128)(2,1)} %shard_map.69), calls=%async_computation.2 | async-start | bytes 4194304 | tf_op jit(solution)/shard_map/all_to_all | solution.py:237
  124.8 1.0 copy-start.3
  125.8 24.2 %copy-start = (bf16[256,32,256]{2,1,0:T(8,128)(2,1)S(1)}, bf16[256,32,256]{2,1,0:T(8,128)(2,1)}, u32[]{:S(2)}) copy-start(bf16[256,32,256]{2,1,0:T(8,128)(2,1)} %shard_map.70.rotated_ref) | copy-start | bytes 12582916
  150.1 23.3 %copy-start.5 = (f32[32]{0:T(128)S(1)}, f32[32]{0:T(128)}, u32[]{:S(2)}) copy-start(f32[32]{0:T(128)} %param.9) | copy-start | bytes 388
  152.0 3.1 %collective-permute-start.9 = (f32[16,256]{1,0:T(8,128)S(1)}, f32[16,256]{1,0:T(8,128)S(1)}, u32[]{:S(2)}, u32[]{:S(2)}) collective-permute-start(f32[16,256]{1,0:T(8,128)S(1)} %dynamic-slice_bitcast_fusion), channel_id=1, source_target_pairs={{0,8},{8,0},{1,9},{9,1},{2,10},{10,2},{3,11},{11,3},{4,12},{12,4},... | collective-permute-start | bytes 49160 | tf_op jit(solution)/shard_map/ppermute | solution.py:241
  172.0 1.3 collective-permute-start.10
  174.6 10.0 %collective-permute-start.11 = (f32[8,128]{1,0:T(8,128)S(1)}, f32[8,128]{1,0:T(8,128)S(1)}, u32[]{:S(2)}, u32[]{:S(2)}) collective-permute-start(f32[8,128]{1,0:T(8,128)S(1)} %broadcast_in_dim.8), channel_id=1, source_target_pairs={{0,1},{1,0},{2,3},{3,2},{4,5},{5,4},{6,7},{7,6},{8,9},{9,8},{10,11... | collective-permute-start | bytes 12296 | tf_op jit(solution)/shard_map/ppermute | solution.py:241
  185.2 55.4 %all-to-all-start.5 = ((bf16[32,32,1024]{2,1,0:T(8,128)(2,1)}), bf16[32,32,1024]{2,1,0:T(8,128)(2,1)S(1)}, u32[]{:S(2)}, u32[]{:S(2)}) async-start(bf16[32,32,1024]{2,1,0:T(8,128)(2,1)} %shard_map.72), calls=%async_computation.5 | async-start | bytes 4194304 | tf_op jit(solution)/shard_map/all_to_all | solution.py:237
  191.5 4.7 %collective-permute-start.14 = (f32[8,128]{1,0:T(8,128)S(1)}, f32[8,128]{1,0:T(8,128)S(1)}, u32[]{:S(2)}, u32[]{:S(2)}) collective-permute-start(f32[8,128]{1,0:T(8,128)S(1)} %broadcast_add_fusion), channel_id=1, source_target_pairs={{0,6},{2,0},{4,2},{6,4},{1,7},{3,1},{5,3},{7,5},{8,14},{10,8},{12,... | collective-permute-start | bytes 12296 | tf_op jit(solution)/shard_map/ppermute | solution.py:252
  194.5 5.1 %collective-permute-start.13 = (f32[8,128]{1,0:T(8,128)S(1)}, f32[8,128]{1,0:T(8,128)S(1)}, u32[]{:S(2)}, u32[]{:S(2)}) collective-permute-start(f32[8,128]{1,0:T(8,128)S(1)} %broadcast_add_fusion), channel_id=1, source_target_pairs={{0,4},{2,6},{4,0},{6,2},{1,5},{3,7},{5,1},{7,3},{8,12},{10,14},{12... | collective-permute-start | bytes 12296 | tf_op jit(solution)/shard_map/ppermute | solution.py:252
  195.2 4.8 %collective-permute-start.12 = (f32[8,128]{1,0:T(8,128)S(1)}, f32[8,128]{1,0:T(8,128)S(1)}, u32[]{:S(2)}, u32[]{:S(2)}) collective-permute-start(f32[8,128]{1,0:T(8,128)S(1)} %broadcast_add_fusion), channel_id=1, source_target_pairs={{0,2},{2,4},{4,6},{6,0},{1,3},{3,5},{5,7},{7,1},{8,10},{10,12},{12... | collective-permute-start | bytes 12296 | tf_op jit(solution)/shard_map/ppermute | solution.py:252
where the time goes:
time: 271 us; the launch traced here: 268 us
  waiting for transfers between devices  90.9 us (34%)
  blocking collectives  86.1 us (32%)
  starting transfers between devices  41.8 us (15%)
  Pallas kernels  36.6 us (14%)
  matrix products  5.91 us (2%)
  local copies, waits for them, and re-layouts  3.15 us (1%)
    all_to_all x4, blocking collectives, exchange(): return lax.all_to_all(value, axis, split_axis=0, concat_axis=0, tiled=True)  86.1 us
    all_to_all x3, waiting for transfers between devices, exchange(): return lax.all_to_all(value, axis, split_axis=0, concat_axis=0, tiled=True)  77.1 us
    all_to_all x3, starting transfers between devices, exchange(): return lax.all_to_all(value, axis, split_axis=0, concat_axis=0, tiled=True)  21 us
    pallas_call x2, Pallas kernels, potential(): pl.pallas_call(potential_kernel, in_specs=[WHOLE, IN_HBM], out_specs=WHOL...  17.7 us
    ppermute x9, starting transfers between devices, ring_sum(): lax.ppermute(value, axis, [(i, (i + shift) % 4) for i in range(4)])  16.9 us
    ppermute x9, waiting for transfers between devices, ring_sum(): lax.ppermute(value, axis, [(i, (i + shift) % 4) for i in range(4)])  9.58 us
    pallas_call x1, Pallas kernels, rotate(): pl.pallas_call(rotate_kernel, in_specs=[IN_HBM, WHOLE], out_specs=IN_HBM,...  8.62 us
    pallas_call x1, Pallas kernels, first_bias(): pl.pallas_call(first_bias_kernel, in_specs=[IN_HBM, WHOLE, WHOLE], out_sp...  8.38 us
  transfers between devices with their start and end apart: 18, of which 12 were waited for; matrix products, arithmetic and copies ran while one was open for 0% of the time, Pallas kernels for 13%

commit v1 on v0

--- a/solution.py
+++ b/solution.py
@@ -246,11 +246,12 @@
     return exchange(jnp.broadcast_to(value[None], (count,) + value.shape), axis)
 
 
+def turn(value, axis, shift):
+    return lax.ppermute(value, axis, [(i, (i + shift) % 4) for i in range(4)])
+
+
 def ring_sum(value, axis):
-    total = value
-    for shift in range(1, 4):
-        total = total + lax.ppermute(value, axis, [(i, (i + shift) % 4) for i in range(4)])
-    return total
+    return value + turn(value, axis, 1) + turn(value, axis, 2) + turn(value, axis, 3)
 
 
 def row_sum(part, by_permutes):
@@ -308,14 +309,15 @@
             sent, trial, phi = lax.optimization_barrier((sent, trial, phi))
             rotated = rotate(cholesky, trial)
         if step == steps - 1:
-            pair_sum = jnp.full((8, 128), jnp.sum(jnp.exp(weights_now)))
-            pair_sum = pair_sum + swap(pair_sum, "zl")
-            sent, pair_sum = lax.optimization_barrier((sent, pair_sum))
+            paired = swap(weights_now, "zl")
+            sent, paired = lax.optimization_barrier((sent, paired))
         sent = exchange(sent, ROW).reshape(orbitals, orbitals)
         if step == 0:
             sent, rotated = lax.optimization_barrier((sent, rotated))
         if step == steps - 1:
-            weight_sum = ring_sum(pair_sum, "y")[0, 0]
+            paired = jnp.concatenate([weights_now, paired])
+            everyone = [paired] + [turn(paired, "y", shift) for shift in range(1, 4)]
+            weight_sum = jnp.sum(jnp.exp(jnp.concatenate(everyone)))
             count = walker_count * lax.axis_size(WALK)
             weights_now = weights_now - jnp.log(weight_sum / count)
         phi = taylor(sent, phi)

time: 271 us -> 269 us (level)
  transfers between devices with their start and end apart: 18 -> 18, of which waited for: 12 -> 12; matrix products, arithmetic and copies ran while one was open for 0% -> 1% of each run, Pallas kernels for 13% -> 13%
where the time goes in v1:
time: 269 us; the launch traced here: 266 us
  waiting for transfers between devices  91.1 us (34%)
  blocking collectives  85.8 us (32%)
  starting transfers between devices  41.8 us (16%)
  Pallas kernels  36.6 us (14%)
  matrix products  5.93 us (2%)
    all_to_all x4, blocking collectives, exchange(): return lax.all_to_all(value, axis, split_axis=0, concat_axis=0, tiled=True)  85.8 us
    all_to_all x3, waiting for transfers between devices, exchange(): return lax.all_to_all(value, axis, split_axis=0, concat_axis=0, tiled=True)  77.4 us
    all_to_all x3, starting transfers between devices, exchange(): return lax.all_to_all(value, axis, split_axis=0, concat_axis=0, tiled=True)  21 us
    pallas_call x2, Pallas kernels, potential(): pl.pallas_call(potential_kernel, in_specs=[WHOLE, IN_HBM], out_specs=WHOL...  17.7 us
    ppermute x9, starting transfers between devices, turn(): return lax.ppermute(value, axis, [(i, (i + shift) % 4) for i in range(4)])  16.9 us
    ppermute x9, waiting for transfers between devices, turn(): return lax.ppermute(value, axis, [(i, (i + shift) % 4) for i in range(4)])  9.5 us
    pallas_call x1, Pallas kernels, rotate(): pl.pallas_call(rotate_kernel, in_specs=[IN_HBM, WHOLE], out_specs=IN_HBM,...  8.62 us
    pallas_call x1, Pallas kernels, first_bias(): pl.pallas_call(first_bias_kernel, in_specs=[IN_HBM, WHOLE, WHOLE], out_sp...  8.37 us
  transfers between devices with their start and end apart: 18, of which 12 were waited for; matrix products, arithmetic and copies ran while one was open for 1% of the time, Pallas kernels for 13%

profile of v1, /device:TPU:6, one launch (start us, length us, event | category | flops | bytes accessed | tf_op | source)
XLA Modules:
  0.0 266.3 jit_solution(10709489167245489115)
XLA Ops:
  1.4 22.2 %all_to_all.35 = bf16[16,32,256]{2,1,0:T(8,128)(2,1)S(1)} all-to-all(bf16[16,32,256]{2,1,0:T(8,128)(2,1)S(1)} %broadcast_in_dim.4), channel_id=1, replica_groups=mesh['x'=4,'zh'=4,'c'=2,'y'=4,'zl'=2] {'x','zh'}, dimensions={0} | all-to-all | bytes 524288 | tf_op jit(solution)/shard_map/all_to_all | solution.py:237
  23.6 6.1 %all-to-all-start.1 = ((bf16[32,32,256]{2,1,0:T(8,128)(2,1)}), bf16[32,32,256]{2,1,0:T(8,128)(2,1)S(1)}, u32[]{:S(2)}, u32[]{:S(2)}) async-start(bf16[32,32,256]{2,1,0:T(8,128)(2,1)} %phi_ref.1), calls=%async_computation.1 | async-start | bytes 1048576 | tf_op jit(solution)/shard_map/all_to_all | solution.py:237
  29.8 8.4 %shard_map.68 = f32[32,256]{1,0:T(8,128)S(1)} custom-call(bf16[256,32,1024]{2,1,0:T(8,128)(2,1)} %chol_hbm.7, bf16[1024,256]{1,0:T(8,128)(2,1)S(1)} %bitcast.46, bf16[32,32,256]{2,1,0:T(8,128)(2,1)S(1)} %copy-done.1), custom_call_target="tpu_custom_call" | custom-call | flops 4294967296 | bytes 16777216 | tf_op jit(solution)/shard_map/pallas_call | solution.py:139
  41.2 2.3 collective-permute-start.2
  45.7 3.6 %collective-permute-start.7 = (f32[16,256]{1,0:T(8,128)S(1)}, f32[16,256]{1,0:T(8,128)S(1)}, u32[]{:S(2)}, u32[]{:S(2)}) collective-permute-start(f32[16,256]{1,0:T(8,128)S(1)} %add_add_fusion.1), channel_id=1, source_target_pairs={{0,48},{16,0},{32,16},{48,32},{1,49},{17,1},{33,17},{49,33},{2,50}... | collective-permute-start | bytes 49160 | tf_op jit(solution)/shard_map/ppermute | solution.py:250
  49.3 2.3 collective-permute-start.6
  51.6 2.4 collective-permute-start.5
  54.0 2.9 %collective-permute-done.6 = f32[16,256]{1,0:T(8,128)S(1)} collective-permute-done((f32[16,256]{1,0:T(8,128)S(1)}, f32[16,256]{1,0:T(8,128)S(1)}, u32[]{:S(2)}, u32[]{:S(2)}) %collective-permute-start.6) | collective-permute-done | bytes 16416 | tf_op jit(solution)/shard_map/ppermute | solution.py:250
  57.6 1.2 collective-permute-done.8
  58.8 8.8 %shard_map.69 = bf16[32,32,1024]{2,1,0:T(8,128)(2,1)} custom-call(bf16[32,256]{1,0:T(8,128)(2,1)S(1)} %fusion.13.mixed_ref, bf16[256,32,1024]{2,1,0:T(8,128)(2,1)} %chol_hbm.7), custom_call_target="tpu_custom_call" | custom-call | tf_op jit(solution)/shard_map/pallas_call | solution.py:222
  67.7 8.7 %all-to-all-start.2 = ((bf16[32,32,1024]{2,1,0:T(8,128)(2,1)}), bf16[32,32,1024]{2,1,0:T(8,128)(2,1)S(1)}, u32[]{:S(2)}, u32[]{:S(2)}) async-start(bf16[32,32,1024]{2,1,0:T(8,128)(2,1)} %shard_map.69), calls=%async_computation.2 | async-start | bytes 4194304 | tf_op jit(solution)/shard_map/all_to_all | solution.py:237
  76.5 8.6 %shard_map.70.rotated_ref = bf16[256,32,256]{2,1,0:T(8,128)(2,1)} custom-call(bf16[256,32,1024]{2,1,0:T(8,128)(2,1)} %chol_hbm.7, bf16[1024,256]{1,0:T(8,128)(2,1)S(1)} %bitcast.47), custom_call_target="tpu_custom_call" | custom-call | flops 4294967296 | bytes 16777216 | tf_op jit(solution)/shard_map/pallas_call | solution.py:182
  85.1 38.5 %all-to-all-done.2 = bf16[32,32,1024]{2,1,0:T(8,128)(2,1)S(1)} async-done(((bf16[32,32,1024]{2,1,0:T(8,128)(2,1)}), bf16[32,32,1024]{2,1,0:T(8,128)(2,1)S(1)}, u32[]{:S(2)}, u32[]{:S(2)}) %all-to-all-start.2) | async-done | bytes 2097184 | tf_op jit(solution)/shard_map/all_to_all | solution.py:237
  126.9 23.2 %all_to_all.36.phi_ref = bf16[32,32,256]{2,1,0:T(8,128)(2,1)S(1)} all-to-all(bf16[32,32,256]{2,1,0:T(8,128)(2,1)S(1)} %bitcast.60), channel_id=1, replica_groups=mesh['x'=4,'zh'=4,'c'=2,'y'=4,'zl'=2] {'x','zh','c'}, dimensions={0} | all-to-all | bytes 1048576 | tf_op jit(solution)/shard_map/all_to_all | solution.py:237
  150.1 1.9 shard_map.71
  152.0 2.3 collective-permute-start.9
  155.2 16.8 %all_to_all.37 = f32[16,16,256]{2,1,0:T(8,128)S(1)} all-to-all(f32[16,16,256]{2,1,0:T(8,128)S(1)} %broadcast_in_dim.5), channel_id=1, replica_groups=mesh['x'=4,'zh'=4,'c'=2,'y'=4,'zl'=2] {'x','zh'}, dimensions={0} | all-to-all | bytes 524288 | tf_op jit(solution)/shard_map/all_to_all | solution.py:237
  172.1 1.2 collective-permute-done.10
  174.5 8.8 %shard_map.72 = bf16[32,32,1024]{2,1,0:T(8,128)(2,1)} custom-call(bf16[32,256]{1,0:T(8,128)(2,1)S(1)} %get-tuple-element.22.mixed_ref, bf16[256,32,1024]{2,1,0:T(8,128)(2,1)} %chol_hbm.7), custom_call_target="tpu_custom_call" | custom-call | tf_op jit(solution)/shard_map/pallas_call | solution.py:222
  183.3 6.2 %all-to-all-start.5 = ((bf16[32,32,1024]{2,1,0:T(8,128)(2,1)}), bf16[32,32,1024]{2,1,0:T(8,128)(2,1)S(1)}, u32[]{:S(2)}, u32[]{:S(2)}) async-start(bf16[32,32,1024]{2,1,0:T(8,128)(2,1)} %shard_map.72), calls=%async_computation.5 | async-start | bytes 4194304 | tf_op jit(solution)/shard_map/all_to_all | solution.py:237
  189.6 3.0 %collective-permute-start.14 = (f32[64]{0:T(128)S(1)}, f32[64]{0:T(128)S(1)}, u32[]{:S(2)}, u32[]{:S(2)}) collective-permute-start(f32[64]{0:T(128)S(1)} %pad_maximum_fusion), channel_id=1, source_target_pairs={{0,6},{2,0},{4,2},{6,4},{1,7},{3,1},{5,3},{7,5},{8,14},{10,8},{12,... | collective-permute-start | bytes 776 | tf_op jit(solution)/shard_map/ppermute | solution.py:250
  194.3 3.4 %collective-permute-done.13 = f32[64]{0:T(128)S(1)} collective-permute-done((f32[64]{0:T(128)S(1)}, f32[64]{0:T(128)S(1)}, u32[]{:S(2)}, u32[]{:S(2)}) %collective-permute-start.13) | collective-permute-done | bytes 288 | tf_op jit(solution)/shard_map/ppermute | solution.py:250
  199.9 38.9 %all-to-all-done.5 = bf16[32,32,1024]{2,1,0:T(8,128)(2,1)S(1)} async-done(((bf16[32,32,1024]{2,1,0:T(8,128)(2,1)}), bf16[32,32,1024]{2,1,0:T(8,128)(2,1)S(1)}, u32[]{:S(2)}, u32[]{:S(2)}) %all-to-all-start.5) | async-done | bytes 2097184 | tf_op jit(solution)/shard_map/all_to_all | solution.py:237
  241.8 23.6 %all_to_all.38 = bf16[32,32,256]{2,1,0:T(8,128)(2,1)S(1)} all-to-all(bf16[32,32,256]{2,1,0:T(8,128)(2,1)S(1)} %bitcast.63), channel_id=1, replica_groups=mesh['x'=4,'zh'=4,'c'=2,'y'=4,'zl'=2] {'x','zh','c'}, dimensions={0} | all-to-all | bytes 1048576 | tf_op jit(solution)/shard_map/all_to_all | solution.py:237
  (59 shorter events, 19.3 us)
Async XLA Ops:
  0.6 29.2 %copy-start.1 = (bf16[32,32,256]{2,1,0:T(8,128)(2,1)S(1)}, bf16[32,32,256]{2,1,0:T(8,128)(2,1)}, u32[]{:S(2)}) copy-start(bf16[32,32,256]{2,1,0:T(8,128)(2,1)} %phi_ref.1) | copy-start | bytes 1572868
  23.6 6.1 %collective-permute-start = (bf16[16,32,256]{2,1,0:T(8,128)(2,1)S(1)}, bf16[16,32,256]{2,1,0:T(8,128)(2,1)S(1)}, u32[]{:S(2)}, u32[]{:S(2)}) collective-permute-start(bf16[16,32,256]{2,1,0:T(8,128)(2,1)S(1)} %all_to_all.35), channel_id=1, source_target_pairs={{0,8},{8,0},{1,9},{9,1},{2,10},{10,2},{3,11},{11,3},{4,12},{12,4},... | collective-permute-start | bytes 786440 | tf_op jit(solution)/shard_map/ppermute | solution.py:241
  23.6 44.0 %all-to-all-start.1 = ((bf16[32,32,256]{2,1,0:T(8,128)(2,1)}), bf16[32,32,256]{2,1,0:T(8,128)(2,1)S(1)}, u32[]{:S(2)}, u32[]{:S(2)}) async-start(bf16[32,32,256]{2,1,0:T(8,128)(2,1)} %phi_ref.1), calls=%async_computation.1 | async-start | bytes 1048576 | tf_op jit(solution)/shard_map/all_to_all | solution.py:237
  29.8 29.0 %copy-start.4 = (f32[2,32,256]{2,1,0:T(8,128)S(1)}, f32[2,32,256]{2,1,0:T(8,128)}, u32[]{:S(2)}) copy-start(f32[2,32,256]{2,1,0:T(8,128)} %param.8) | copy-start | bytes 196612
  38.2 1.3 collective-permute-start.1
  39.5 5.1 %collective-permute-start.4 = (f32[16,256]{1,0:T(8,128)S(1)}, f32[16,256]{1,0:T(8,128)S(1)}, u32[]{:S(2)}, u32[]{:S(2)}) collective-permute-start(f32[16,256]{1,0:T(8,128)S(1)} %bitcast_add_fusion.1), channel_id=1, source_target_pairs={{0,192},{64,0},{128,64},{192,128},{1,193},{65,1},{129,65},{193,129... | collective-permute-start | bytes 49160 | tf_op jit(solution)/shard_map/ppermute | solution.py:250
  40.3 5.4 %collective-permute-start.3 = (f32[16,256]{1,0:T(8,128)S(1)}, f32[16,256]{1,0:T(8,128)S(1)}, u32[]{:S(2)}, u32[]{:S(2)}) collective-permute-start(f32[16,256]{1,0:T(8,128)S(1)} %bitcast_add_fusion.1), channel_id=1, source_target_pairs={{0,128},{64,192},{128,0},{192,64},{1,129},{65,193},{129,1},{193,65... | collective-permute-start | bytes 49160 | tf_op jit(solution)/shard_map/ppermute | solution.py:250
  41.2 4.5 %collective-permute-start.2 = (f32[16,256]{1,0:T(8,128)S(1)}, f32[16,256]{1,0:T(8,128)S(1)}, u32[]{:S(2)}, u32[]{:S(2)}) collective-permute-start(f32[16,256]{1,0:T(8,128)S(1)} %bitcast_add_fusion.1), channel_id=1, source_target_pairs={{0,64},{64,128},{128,192},{192,0},{1,65},{65,129},{129,193},{193,1... | collective-permute-start | bytes 49160 | tf_op jit(solution)/shard_map/ppermute | solution.py:250
  45.7 8.3 %collective-permute-start.7 = (f32[16,256]{1,0:T(8,128)S(1)}, f32[16,256]{1,0:T(8,128)S(1)}, u32[]{:S(2)}, u32[]{:S(2)}) collective-permute-start(f32[16,256]{1,0:T(8,128)S(1)} %add_add_fusion.1), channel_id=1, source_target_pairs={{0,48},{16,0},{32,16},{48,32},{1,49},{17,1},{33,17},{49,33},{2,50}... | collective-permute-start | bytes 49160 | tf_op jit(solution)/shard_map/ppermute | solution.py:250
  49.3 7.6 %collective-permute-start.6 = (f32[16,256]{1,0:T(8,128)S(1)}, f32[16,256]{1,0:T(8,128)S(1)}, u32[]{:S(2)}, u32[]{:S(2)}) collective-permute-start(f32[16,256]{1,0:T(8,128)S(1)} %add_add_fusion.1), channel_id=1, source_target_pairs={{0,32},{16,48},{32,0},{48,16},{1,33},{17,49},{33,1},{49,17},{2,34}... | collective-permute-start | bytes 49160 | tf_op jit(solution)/shard_map/ppermute | solution.py:250
  51.6 5.9 %collective-permute-start.5 = (f32[16,256]{1,0:T(8,128)S(1)}, f32[16,256]{1,0:T(8,128)S(1)}, u32[]{:S(2)}, u32[]{:S(2)}) collective-permute-start(f32[16,256]{1,0:T(8,128)S(1)} %add_add_fusion.1), channel_id=1, source_target_pairs={{0,16},{16,32},{32,48},{48,0},{1,17},{17,33},{33,49},{49,1},{2,18}... | collective-permute-start | bytes 49160 | tf_op jit(solution)/shard_map/ppermute | solution.py:250
  57.5 1.3 collective-permute-start.8
  67.7 55.9 %copy-start.2 = (bf16[32,32,256]{2,1,0:T(8,128)(2,1)}, bf16[32,32,256]{2,1,0:T(8,128)(2,1)S(1)}, u32[]{:S(2)}) copy-start(bf16[32,32,256]{2,1,0:T(8,128)(2,1)S(1)} %all-to-all-done.1) | copy-start | bytes 1572868
  67.7 55.9 %all-to-all-start.2 = ((bf16[32,32,1024]{2,1,0:T(8,128)(2,1)}), bf16[32,32,1024]{2,1,0:T(8,128)(2,1)S(1)}, u32[]{:S(2)}, u32[]{:S(2)}) async-start(bf16[32,32,1024]{2,1,0:T(8,128)(2,1)} %shard_map.69), calls=%async_computation.2 | async-start | bytes 4194304 | tf_op jit(solution)/shard_map/all_to_all | solution.py:237
  125.1 1.0 copy-start.3
  126.1 24.0 %copy-start = (bf16[256,32,256]{2,1,0:T(8,128)(2,1)S(1)}, bf16[256,32,256]{2,1,0:T(8,128)(2,1)}, u32[]{:S(2)}) copy-start(bf16[256,32,256]{2,1,0:T(8,128)(2,1)} %shard_map.70.rotated_ref) | copy-start | bytes 12582916
  150.1 23.3 %copy-start.5 = (f32[32]{0:T(128)S(1)}, f32[32]{0:T(128)}, u32[]{:S(2)}) copy-start(f32[32]{0:T(128)} %param.9) | copy-start | bytes 388
  152.0 3.1 %collective-permute-start.9 = (f32[16,256]{1,0:T(8,128)S(1)}, f32[16,256]{1,0:T(8,128)S(1)}, u32[]{:S(2)}, u32[]{:S(2)}) collective-permute-start(f32[16,256]{1,0:T(8,128)S(1)} %dynamic-slice_bitcast_fusion), channel_id=1, source_target_pairs={{0,8},{8,0},{1,9},{9,1},{2,10},{10,2},{3,11},{11,3},{4,12},{12,4},... | collective-permute-start | bytes 49160 | tf_op jit(solution)/shard_map/ppermute | solution.py:241
  172.0 1.3 collective-permute-start.10
  173.4 9.9 %collective-permute-start.11 = (f32[32]{0:T(128)S(1)}, f32[32]{0:T(128)S(1)}, u32[]{:S(2)}, u32[]{:S(2)}) collective-permute-start(f32[32]{0:T(128)S(1)} %add_add_fusion.2), channel_id=1, source_target_pairs={{0,1},{1,0},{2,3},{3,2},{4,5},{5,4},{6,7},{7,6},{8,9},{9,8},{10,11... | collective-permute-start | bytes 392 | tf_op jit(solution)/shard_map/ppermute | solution.py:241
  183.3 55.5 %all-to-all-start.5 = ((bf16[32,32,1024]{2,1,0:T(8,128)(2,1)}), bf16[32,32,1024]{2,1,0:T(8,128)(2,1)S(1)}, u32[]{:S(2)}, u32[]{:S(2)}) async-start(bf16[32,32,1024]{2,1,0:T(8,128)(2,1)} %shard_map.72), calls=%async_computation.5 | async-start | bytes 4194304 | tf_op jit(solution)/shard_map/all_to_all | solution.py:237
  189.6 4.6 %collective-permute-start.14 = (f32[64]{0:T(128)S(1)}, f32[64]{0:T(128)S(1)}, u32[]{:S(2)}, u32[]{:S(2)}) collective-permute-start(f32[64]{0:T(128)S(1)} %pad_maximum_fusion), channel_id=1, source_target_pairs={{0,6},{2,0},{4,2},{6,4},{1,7},{3,1},{5,3},{7,5},{8,14},{10,8},{12,... | collective-permute-start | bytes 776 | tf_op jit(solution)/shard_map/ppermute | solution.py:250
  192.7 5.0 %collective-permute-start.13 = (f32[64]{0:T(128)S(1)}, f32[64]{0:T(128)S(1)}, u32[]{:S(2)}, u32[]{:S(2)}) collective-permute-start(f32[64]{0:T(128)S(1)} %pad_maximum_fusion), channel_id=1, source_target_pairs={{0,4},{2,6},{4,0},{6,2},{1,5},{3,7},{5,1},{7,3},{8,12},{10,14},{12... | collective-permute-start | bytes 776 | tf_op jit(solution)/shard_map/ppermute | solution.py:250
  193.3 4.8 %collective-permute-start.12 = (f32[64]{0:T(128)S(1)}, f32[64]{0:T(128)S(1)}, u32[]{:S(2)}, u32[]{:S(2)}) collective-permute-start(f32[64]{0:T(128)S(1)} %pad_maximum_fusion), channel_id=1, source_target_pairs={{0,2},{2,4},{4,6},{6,0},{1,3},{3,5},{5,7},{7,1},{8,10},{10,12},{12... | collective-permute-start | bytes 776 | tf_op jit(solution)/shard_map/ppermute | solution.py:250

commit v2 on v1

--- a/solution.py
+++ b/solution.py
@@ -314,15 +314,14 @@
         sent = exchange(sent, ROW).reshape(orbitals, orbitals)
         if step == 0:
             sent, rotated = lax.optimization_barrier((sent, rotated))
+        phi = taylor(sent, phi)
         if step == steps - 1:
+            phi, paired = lax.optimization_barrier((phi, paired))
             paired = jnp.concatenate([weights_now, paired])
             everyone = [paired] + [turn(paired, "y", shift) for shift in range(1, 4)]
             weight_sum = jnp.sum(jnp.exp(jnp.concatenate(everyone)))
             count = walker_count * lax.axis_size(WALK)
             weights_now = weights_now - jnp.log(weight_sum / count)
-        phi = taylor(sent, phi)
-        if step == steps - 1:
-            phi, weights_now = lax.optimization_barrier((phi, weights_now))
         phi_rows = exchange(phi.reshape(walker_count, rows, electrons), ROW)
         if step < steps - 1:
             part = bias(rotated, phi_rows)

time: 269 us -> 268 us (level)
  waiting for transfers between devices: 91.1 us -> 57.6 us
  blocking collectives: 85.8 us -> 119 us
    all_to_all x3, waiting for transfers between devices: 77.4 us -> 43.9 us  [exchange(): return lax.all_to_all(value, axis, split_axis=0, concat_axis=0, tiled=True)]
    all_to_all x4, blocking collectives: 85.8 us -> 119 us  [exchange(): return lax.all_to_all(value, axis, split_axis=0, concat_axis=0, tiled=True)]
where the time goes in v2:
time: 268 us; the launch traced here: 265 us
  blocking collectives  119 us (44%)
  waiting for transfers between devices  57.6 us (21%)
  starting transfers between devices  42 us (16%)
  Pallas kernels  35.2 us (13%)
  matrix products  6.64 us (2%)
    all_to_all x4, blocking collectives, exchange(): return lax.all_to_all(value, axis, split_axis=0, concat_axis=0, tiled=True)  119 us
    all_to_all x3, waiting for transfers between devices, exchange(): return lax.all_to_all(value, axis, split_axis=0, concat_axis=0, tiled=True)  43.9 us
    all_to_all x3, starting transfers between devices, exchange(): return lax.all_to_all(value, axis, split_axis=0, concat_axis=0, tiled=True)  21.3 us
    ppermute x9, starting transfers between devices, turn(): return lax.ppermute(value, axis, [(i, (i + shift) % 4) for i in range(4)])  16.8 us
    pallas_call x2, Pallas kernels, potential(): pl.pallas_call(potential_kernel, in_specs=[WHOLE, IN_HBM], out_specs=WHOL...  16.3 us
    ppermute x9, waiting for transfers between devices, turn(): return lax.ppermute(value, axis, [(i, (i + shift) % 4) for i in range(4)])  9.51 us
    pallas_call x1, Pallas kernels, rotate(): pl.pallas_call(rotate_kernel, in_specs=[IN_HBM, WHOLE], out_specs=IN_HBM,...  8.62 us
    pallas_call x1, Pallas kernels, first_bias(): pl.pallas_call(first_bias_kernel, in_specs=[IN_HBM, WHOLE, WHOLE], out_sp...  8.38 us
  transfers between devices with their start and end apart: 18, of which 12 were waited for; matrix products, arithmetic and copies ran while one was open for 1% of the time, Pallas kernels for 13%

profile of v2, /device:TPU:6, one launch (start us, length us, event | category | flops | bytes accessed | tf_op | source)
XLA Modules:
  0.0 264.8 jit_solution(9924711052499815317)
XLA Ops:
  1.4 22.2 %all_to_all.35 = bf16[16,32,256]{2,1,0:T(8,128)(2,1)S(1)} all-to-all(bf16[16,32,256]{2,1,0:T(8,128)(2,1)S(1)} %broadcast_in_dim.4), channel_id=1, replica_groups=mesh['x'=4,'zh'=4,'c'=2,'y'=4,'zl'=2] {'x','zh'}, dimensions={0} | all-to-all | bytes 524288 | tf_op jit(solution)/shard_map/all_to_all | solution.py:237
  23.6 6.1 %all-to-all-start.1 = ((bf16[32,32,256]{2,1,0:T(8,128)(2,1)}), bf16[32,32,256]{2,1,0:T(8,128)(2,1)S(1)}, u32[]{:S(2)}, u32[]{:S(2)}) async-start(bf16[32,32,256]{2,1,0:T(8,128)(2,1)} %phi_ref.1), calls=%async_computation.1 | async-start | bytes 1048576 | tf_op jit(solution)/shard_map/all_to_all | solution.py:237
  29.8 8.4 %shard_map.68 = f32[32,256]{1,0:T(8,128)S(1)} custom-call(bf16[256,32,1024]{2,1,0:T(8,128)(2,1)} %chol_hbm.7, bf16[1024,256]{1,0:T(8,128)(2,1)S(1)} %bitcast.46, bf16[32,32,256]{2,1,0:T(8,128)(2,1)S(1)} %copy-done.1), custom_call_target="tpu_custom_call" | custom-call | flops 4294967296 | bytes 16777216 | tf_op jit(solution)/shard_map/pallas_call | solution.py:139
  41.2 2.3 collective-permute-start.2
  45.7 3.6 %collective-permute-start.7 = (f32[16,256]{1,0:T(8,128)S(1)}, f32[16,256]{1,0:T(8,128)S(1)}, u32[]{:S(2)}, u32[]{:S(2)}) collective-permute-start(f32[16,256]{1,0:T(8,128)S(1)} %add_add_fusion.1), channel_id=1, source_target_pairs={{0,48},{16,0},{32,16},{48,32},{1,49},{17,1},{33,17},{49,33},{2,50}... | collective-permute-start | bytes 49160 | tf_op jit(solution)/shard_map/ppermute | solution.py:250
  49.3 2.3 collective-permute-start.6
  51.6 2.4 collective-permute-start.5
  54.0 2.9 %collective-permute-done.6 = f32[16,256]{1,0:T(8,128)S(1)} collective-permute-done((f32[16,256]{1,0:T(8,128)S(1)}, f32[16,256]{1,0:T(8,128)S(1)}, u32[]{:S(2)}, u32[]{:S(2)}) %collective-permute-start.6) | collective-permute-done | bytes 16416 | tf_op jit(solution)/shard_map/ppermute | solution.py:250
  57.6 1.2 collective-permute-done.8
  58.8 8.8 %shard_map.69 = bf16[32,32,1024]{2,1,0:T(8,128)(2,1)} custom-call(bf16[32,256]{1,0:T(8,128)(2,1)S(1)} %fusion.13.mixed_ref, bf16[256,32,1024]{2,1,0:T(8,128)(2,1)} %chol_hbm.7), custom_call_target="tpu_custom_call" | custom-call | tf_op jit(solution)/shard_map/pallas_call | solution.py:222
  67.7 8.7 %all-to-all-start.2 = ((bf16[32,32,1024]{2,1,0:T(8,128)(2,1)}), bf16[32,32,1024]{2,1,0:T(8,128)(2,1)S(1)}, u32[]{:S(2)}, u32[]{:S(2)}) async-start(bf16[32,32,1024]{2,1,0:T(8,128)(2,1)} %shard_map.69), calls=%async_computation.2 | async-start | bytes 4194304 | tf_op jit(solution)/shard_map/all_to_all | solution.py:237
  76.4 8.6 %shard_map.70.rotated_ref = bf16[256,32,256]{2,1,0:T(8,128)(2,1)} custom-call(bf16[256,32,1024]{2,1,0:T(8,128)(2,1)} %chol_hbm.7, bf16[1024,256]{1,0:T(8,128)(2,1)S(1)} %bitcast.47), custom_call_target="tpu_custom_call" | custom-call | flops 4294967296 | bytes 16777216 | tf_op jit(solution)/shard_map/pallas_call | solution.py:182
  85.1 38.2 %all-to-all-done.2 = bf16[32,32,1024]{2,1,0:T(8,128)(2,1)S(1)} async-done(((bf16[32,32,1024]{2,1,0:T(8,128)(2,1)}), bf16[32,32,1024]{2,1,0:T(8,128)(2,1)S(1)}, u32[]{:S(2)}, u32[]{:S(2)}) %all-to-all-start.2) | async-done | bytes 2097184 | tf_op jit(solution)/shard_map/all_to_all | solution.py:237
  126.3 23.4 %all_to_all.36.phi_ref = bf16[32,32,256]{2,1,0:T(8,128)(2,1)S(1)} all-to-all(bf16[32,32,256]{2,1,0:T(8,128)(2,1)S(1)} %bitcast.60), channel_id=1, replica_groups=mesh['x'=4,'zh'=4,'c'=2,'y'=4,'zl'=2] {'x','zh','c'}, dimensions={0} | all-to-all | bytes 1048576 | tf_op jit(solution)/shard_map/all_to_all | solution.py:237
  149.7 1.9 shard_map.71
  151.7 2.3 collective-permute-start.9
  154.9 16.8 %all_to_all.37 = f32[16,16,256]{2,1,0:T(8,128)S(1)} all-to-all(f32[16,16,256]{2,1,0:T(8,128)S(1)} %broadcast_in_dim.5), channel_id=1, replica_groups=mesh['x'=4,'zh'=4,'c'=2,'y'=4,'zl'=2] {'x','zh'}, dimensions={0} | all-to-all | bytes 524288 | tf_op jit(solution)/shard_map/all_to_all | solution.py:237
  174.2 7.5 %shard_map.72 = bf16[32,32,1024]{2,1,0:T(8,128)(2,1)S(1)} custom-call(bf16[32,256]{1,0:T(8,128)(2,1)S(1)} %get-tuple-element.22.mixed_ref, bf16[256,32,1024]{2,1,0:T(8,128)(2,1)} %chol_hbm.7), custom_call_target="tpu_custom_call" | custom-call | tf_op jit(solution)/shard_map/pallas_call | solution.py:222
  181.7 56.2 %all_to_all.38 = bf16[32,32,1024]{2,1,0:T(8,128)(2,1)S(1)} all-to-all(bf16[32,32,1024]{2,1,0:T(8,128)(2,1)S(1)} %shard_map.72), channel_id=1, replica_groups=mesh['x'=4,'zh'=4,'c'=2,'y'=4,'zl'=2] {'x','zh','c'}, dimensions={0} | all-to-all | bytes 4194304 | tf_op jit(solution)/shard_map/all_to_all | solution.py:237
  240.0 1.5 fusion.3
  241.5 6.5 %all-to-all-start.6 = ((bf16[32,32,256]{2,1,0:T(8,128)(2,1)}), bf16[32,32,256]{2,1,0:T(8,128)(2,1)S(1)}, u32[]{:S(2)}, u32[]{:S(2)}) async-start(bf16[32,32,256]{2,1,0:T(8,128)(2,1)} %bitcast.15), calls=%async_computation.6 | async-start | bytes 1048576 | tf_op jit(solution)/shard_map/all_to_all | solution.py:237
  248.1 3.0 %collective-permute-start.14 = (f32[64]{0:T(128)S(1)}, f32[64]{0:T(128)S(1)}, u32[]{:S(2)}, u32[]{:S(2)}) collective-permute-start(f32[64]{0:T(128)S(1)} %pad_maximum_fusion), channel_id=1, source_target_pairs={{0,6},{2,0},{4,2},{6,4},{1,7},{3,1},{5,3},{7,5},{8,14},{10,8},{12,... | collective-permute-start | bytes 776 | tf_op jit(solution)/shard_map/ppermute | solution.py:250
  252.7 3.4 %collective-permute-done.13 = f32[64]{0:T(128)S(1)} collective-permute-done((f32[64]{0:T(128)S(1)}, f32[64]{0:T(128)S(1)}, u32[]{:S(2)}, u32[]{:S(2)}) %collective-permute-start.13) | collective-permute-done | bytes 288 | tf_op jit(solution)/shard_map/ppermute | solution.py:250
  258.3 5.6 %all-to-all-done.6 = bf16[32,32,256]{2,1,0:T(8,128)(2,1)S(1)} async-done(((bf16[32,32,256]{2,1,0:T(8,128)(2,1)}), bf16[32,32,256]{2,1,0:T(8,128)(2,1)S(1)}, u32[]{:S(2)}, u32[]{:S(2)}) %all-to-all-start.6) | async-done | bytes 524320 | tf_op jit(solution)/shard_map/all_to_all | solution.py:237
  (55 shorter events, 19.3 us)
Async XLA Ops:
  0.6 29.2 %copy-start.1 = (bf16[32,32,256]{2,1,0:T(8,128)(2,1)S(1)}, bf16[32,32,256]{2,1,0:T(8,128)(2,1)}, u32[]{:S(2)}) copy-start(bf16[32,32,256]{2,1,0:T(8,128)(2,1)} %phi_ref.1) | copy-start | bytes 1572868
  23.6 6.1 %collective-permute-start = (bf16[16,32,256]{2,1,0:T(8,128)(2,1)S(1)}, bf16[16,32,256]{2,1,0:T(8,128)(2,1)S(1)}, u32[]{:S(2)}, u32[]{:S(2)}) collective-permute-start(bf16[16,32,256]{2,1,0:T(8,128)(2,1)S(1)} %all_to_all.35), channel_id=1, source_target_pairs={{0,8},{8,0},{1,9},{9,1},{2,10},{10,2},{3,11},{11,3},{4,12},{12,4},... | collective-permute-start | bytes 786440 | tf_op jit(solution)/shard_map/ppermute | solution.py:241
  23.6 44.0 %all-to-all-start.1 = ((bf16[32,32,256]{2,1,0:T(8,128)(2,1)}), bf16[32,32,256]{2,1,0:T(8,128)(2,1)S(1)}, u32[]{:S(2)}, u32[]{:S(2)}) async-start(bf16[32,32,256]{2,1,0:T(8,128)(2,1)} %phi_ref.1), calls=%async_computation.1 | async-start | bytes 1048576 | tf_op jit(solution)/shard_map/all_to_all | solution.py:237
  29.8 29.0 %copy-start.2 = (f32[2,32,256]{2,1,0:T(8,128)S(1)}, f32[2,32,256]{2,1,0:T(8,128)}, u32[]{:S(2)}) copy-start(f32[2,32,256]{2,1,0:T(8,128)} %param.8) | copy-start | bytes 196612
  38.2 1.3 collective-permute-start.1
  39.5 5.1 %collective-permute-start.4 = (f32[16,256]{1,0:T(8,128)S(1)}, f32[16,256]{1,0:T(8,128)S(1)}, u32[]{:S(2)}, u32[]{:S(2)}) collective-permute-start(f32[16,256]{1,0:T(8,128)S(1)} %bitcast_add_fusion.1), channel_id=1, source_target_pairs={{0,192},{64,0},{128,64},{192,128},{1,193},{65,1},{129,65},{193,129... | collective-permute-start | bytes 49160 | tf_op jit(solution)/shard_map/ppermute | solution.py:250
  40.3 5.4 %collective-permute-start.3 = (f32[16,256]{1,0:T(8,128)S(1)}, f32[16,256]{1,0:T(8,128)S(1)}, u32[]{:S(2)}, u32[]{:S(2)}) collective-permute-start(f32[16,256]{1,0:T(8,128)S(1)} %bitcast_add_fusion.1), channel_id=1, source_target_pairs={{0,128},{64,192},{128,0},{192,64},{1,129},{65,193},{129,1},{193,65... | collective-permute-start | bytes 49160 | tf_op jit(solution)/shard_map/ppermute | solution.py:250
  41.2 4.5 %collective-permute-start.2 = (f32[16,256]{1,0:T(8,128)S(1)}, f32[16,256]{1,0:T(8,128)S(1)}, u32[]{:S(2)}, u32[]{:S(2)}) collective-permute-start(f32[16,256]{1,0:T(8,128)S(1)} %bitcast_add_fusion.1), channel_id=1, source_target_pairs={{0,64},{64,128},{128,192},{192,0},{1,65},{65,129},{129,193},{193,1... | collective-permute-start | bytes 49160 | tf_op jit(solution)/shard_map/ppermute | solution.py:250
  45.7 8.3 %collective-permute-start.7 = (f32[16,256]{1,0:T(8,128)S(1)}, f32[16,256]{1,0:T(8,128)S(1)}, u32[]{:S(2)}, u32[]{:S(2)}) collective-permute-start(f32[16,256]{1,0:T(8,128)S(1)} %add_add_fusion.1), channel_id=1, source_target_pairs={{0,48},{16,0},{32,16},{48,32},{1,49},{17,1},{33,17},{49,33},{2,50}... | collective-permute-start | bytes 49160 | tf_op jit(solution)/shard_map/ppermute | solution.py:250
  49.3 7.6 %collective-permute-start.6 = (f32[16,256]{1,0:T(8,128)S(1)}, f32[16,256]{1,0:T(8,128)S(1)}, u32[]{:S(2)}, u32[]{:S(2)}) collective-permute-start(f32[16,256]{1,0:T(8,128)S(1)} %add_add_fusion.1), channel_id=1, source_target_pairs={{0,32},{16,48},{32,0},{48,16},{1,33},{17,49},{33,1},{49,17},{2,34}... | collective-permute-start | bytes 49160 | tf_op jit(solution)/shard_map/ppermute | solution.py:250
  51.6 5.9 %collective-permute-start.5 = (f32[16,256]{1,0:T(8,128)S(1)}, f32[16,256]{1,0:T(8,128)S(1)}, u32[]{:S(2)}, u32[]{:S(2)}) collective-permute-start(f32[16,256]{1,0:T(8,128)S(1)} %add_add_fusion.1), channel_id=1, source_target_pairs={{0,16},{16,32},{32,48},{48,0},{1,17},{17,33},{33,49},{49,1},{2,18}... | collective-permute-start | bytes 49160 | tf_op jit(solution)/shard_map/ppermute | solution.py:250
  57.5 1.3 collective-permute-start.8
  67.7 55.6 %all-to-all-start.2 = ((bf16[32,32,1024]{2,1,0:T(8,128)(2,1)}), bf16[32,32,1024]{2,1,0:T(8,128)(2,1)S(1)}, u32[]{:S(2)}, u32[]{:S(2)}) async-start(bf16[32,32,1024]{2,1,0:T(8,128)(2,1)} %shard_map.69), calls=%async_computation.2 | async-start | bytes 4194304 | tf_op jit(solution)/shard_map/all_to_all | solution.py:237
  125.5 24.2 %copy-start = (bf16[256,32,256]{2,1,0:T(8,128)(2,1)S(1)}, bf16[256,32,256]{2,1,0:T(8,128)(2,1)}, u32[]{:S(2)}) copy-start(bf16[256,32,256]{2,1,0:T(8,128)(2,1)} %shard_map.70.rotated_ref) | copy-start | bytes 12582916
  149.7 23.3 %copy-start.3 = (f32[32]{0:T(128)S(1)}, f32[32]{0:T(128)}, u32[]{:S(2)}) copy-start(f32[32]{0:T(128)} %param.9) | copy-start | bytes 388
  151.7 3.1 %collective-permute-start.9 = (f32[16,256]{1,0:T(8,128)S(1)}, f32[16,256]{1,0:T(8,128)S(1)}, u32[]{:S(2)}, u32[]{:S(2)}) collective-permute-start(f32[16,256]{1,0:T(8,128)S(1)} %dynamic-slice_bitcast_fusion), channel_id=1, source_target_pairs={{0,8},{8,0},{1,9},{9,1},{2,10},{10,2},{3,11},{11,3},{4,12},{12,4},... | collective-permute-start | bytes 49160 | tf_op jit(solution)/shard_map/ppermute | solution.py:241
  171.6 1.3 collective-permute-start.10
  173.1 8.6 %collective-permute-start.11 = (f32[32]{0:T(128)S(1)}, f32[32]{0:T(128)S(1)}, u32[]{:S(2)}, u32[]{:S(2)}) collective-permute-start(f32[32]{0:T(128)S(1)} %add_add_fusion.2), channel_id=1, source_target_pairs={{0,1},{1,0},{2,3},{3,2},{4,5},{5,4},{6,7},{7,6},{8,9},{9,8},{10,11... | collective-permute-start | bytes 392 | tf_op jit(solution)/shard_map/ppermute | solution.py:241
  241.5 22.4 %all-to-all-start.6 = ((bf16[32,32,256]{2,1,0:T(8,128)(2,1)}), bf16[32,32,256]{2,1,0:T(8,128)(2,1)S(1)}, u32[]{:S(2)}, u32[]{:S(2)}) async-start(bf16[32,32,256]{2,1,0:T(8,128)(2,1)} %bitcast.15), calls=%async_computation.6 | async-start | bytes 1048576 | tf_op jit(solution)/shard_map/all_to_all | solution.py:237
  248.1 4.6 %collective-permute-start.14 = (f32[64]{0:T(128)S(1)}, f32[64]{0:T(128)S(1)}, u32[]{:S(2)}, u32[]{:S(2)}) collective-permute-start(f32[64]{0:T(128)S(1)} %pad_maximum_fusion), channel_id=1, source_target_pairs={{0,6},{2,0},{4,2},{6,4},{1,7},{3,1},{5,3},{7,5},{8,14},{10,8},{12,... | collective-permute-start | bytes 776 | tf_op jit(solution)/shard_map/ppermute | solution.py:250
  251.1 5.0 %collective-permute-start.13 = (f32[64]{0:T(128)S(1)}, f32[64]{0:T(128)S(1)}, u32[]{:S(2)}, u32[]{:S(2)}) collective-permute-start(f32[64]{0:T(128)S(1)} %pad_maximum_fusion), channel_id=1, source_target_pairs={{0,4},{2,6},{4,0},{6,2},{1,5},{3,7},{5,1},{7,3},{8,12},{10,14},{12... | collective-permute-start | bytes 776 | tf_op jit(solution)/shard_map/ppermute | solution.py:250
  251.7 4.8 %collective-permute-start.12 = (f32[64]{0:T(128)S(1)}, f32[64]{0:T(128)S(1)}, u32[]{:S(2)}, u32[]{:S(2)}) collective-permute-start(f32[64]{0:T(128)S(1)} %pad_maximum_fusion), channel_id=1, source_target_pairs={{0,2},{2,4},{4,6},{6,0},{1,3},{3,5},{5,7},{7,1},{8,10},{10,12},{12... | collective-permute-start | bytes 776 | tf_op jit(solution)/shard_map/ppermute | solution.py:250

commit v3 on v2

--- a/solution.py
+++ b/solution.py
@@ -281,14 +281,35 @@
     return both.reshape(-1, rows.shape[-1])
 
 
+def taylor_kernel(potential_ref, walker_ref, out_ref, term_ref, summed_ref):
+    orbitals = potential_ref.shape[0]
+    count = 512
+    for degree in range(1, 5):
+        held = walker_ref if degree == 1 else term_ref.at[degree % 2]
+        for low in range(0, orbitals, count):
+            at = slice(low, low + count)
+            next_term = dot(potential_ref[at, :], held[...]) / degree
+            before = walker_ref[at, :].astype(jnp.float32) if degree == 1 else summed_ref[at, :]
+            if degree < 4:
+                summed_ref[at, :] = before + next_term
+                term_ref[(degree + 1) % 2, at, :] = next_term.astype(jnp.bfloat16)
+            else:
+                out_ref[at, :] = (before + next_term).astype(jnp.bfloat16)
+
+
 def taylor(potential, walker):
-    summed = walker.astype(jnp.float32)
-    power_term = walker
-    for degree in range(1, 5):
-        next_term = jnp.dot(potential, power_term, preferred_element_type=jnp.float32) / degree
-        summed = summed + next_term
-        power_term = next_term.astype(jnp.bfloat16)
-    return summed.astype(jnp.bfloat16)
+    return pl.pallas_call(
+        taylor_kernel,
+        in_specs=[WHOLE] * 2,
+        out_specs=WHOLE,
+        out_shape=jax.ShapeDtypeStruct(walker.shape, jnp.bfloat16),
+        scratch_shapes=[
+            pltpu.VMEM((2,) + walker.shape, jnp.bfloat16),
+            pltpu.VMEM(walker.shape, jnp.float32),
+        ],
+        compiler_params=params(12),
+        cost_estimate=cost(2**31, 2**22),
+    )(potential, walker)
 
 
 def shards(cholesky, walkers, trial_orbitals, fields, log_weights):

time: 268 us -> 268 us (level)
  matrix products: 6.64 us -> 0 us
  Pallas kernels: 35.2 us -> 41.1 us
    dot_general x8 -> x0, matrix products: 6.64 us -> none  [taylor(): jnp.dot(potential, power_term, preferred_element_type=jnp.float32) / degree]
    pallas_call x0 -> x2, Pallas kernels: none -> 5.94 us  [taylor(): pl.pallas_call(taylor_kernel, in_specs=[WHOLE] * 2, out_specs=WHOLE, out_...]
where the time goes in v3:
time: 268 us; the launch traced here: 264 us
  blocking collectives  118 us (44%)
  waiting for transfers between devices  57.5 us (21%)
  starting transfers between devices  42.2 us (16%)
  Pallas kernels  41.1 us (15%)
    all_to_all x4, blocking collectives, exchange(): return lax.all_to_all(value, axis, split_axis=0, concat_axis=0, tiled=True)  118 us
    all_to_all x3, waiting for transfers between devices, exchange(): return lax.all_to_all(value, axis, split_axis=0, concat_axis=0, tiled=True)  43.8 us
    all_to_all x3, starting transfers between devices, exchange(): return lax.all_to_all(value, axis, split_axis=0, concat_axis=0, tiled=True)  21.3 us
    ppermute x9, starting transfers between devices, turn(): return lax.ppermute(value, axis, [(i, (i + shift) % 4) for i in range(4)])  16.8 us
    pallas_call x2, Pallas kernels, potential(): pl.pallas_call(potential_kernel, in_specs=[WHOLE, IN_HBM], out_specs=WHOL...  16.3 us
    ppermute x9, waiting for transfers between devices, turn(): return lax.ppermute(value, axis, [(i, (i + shift) % 4) for i in range(4)])  9.51 us
    pallas_call x1, Pallas kernels, rotate(): pl.pallas_call(rotate_kernel, in_specs=[IN_HBM, WHOLE], out_specs=IN_HBM,...  8.62 us
    pallas_call x1, Pallas kernels, first_bias(): pl.pallas_call(first_bias_kernel, in_specs=[IN_HBM, WHOLE, WHOLE], out_sp...  8.38 us
  transfers between devices with their start and end apart: 18, of which 12 were waited for; matrix products, arithmetic and copies ran while one was open for 1% of the time, Pallas kernels for 13%

profile of v3, /device:TPU:6, one launch (start us, length us, event | category | flops | bytes accessed | tf_op | source)
XLA Modules:
  0.0 264.0 jit_solution(7268912885201118670)
XLA Ops:
  1.4 22.2 %all_to_all.35 = bf16[16,32,256]{2,1,0:T(8,128)(2,1)S(1)} all-to-all(bf16[16,32,256]{2,1,0:T(8,128)(2,1)S(1)} %broadcast_in_dim.4), channel_id=1, replica_groups=mesh['x'=4,'zh'=4,'c'=2,'y'=4,'zl'=2] {'x','zh'}, dimensions={0} | all-to-all | bytes 524288 | tf_op jit(solution)/shard_map/all_to_all | solution.py:237
  23.6 6.1 %all-to-all-start.1 = ((bf16[32,32,256]{2,1,0:T(8,128)(2,1)}), bf16[32,32,256]{2,1,0:T(8,128)(2,1)S(1)}, u32[]{:S(2)}, u32[]{:S(2)}) async-start(bf16[32,32,256]{2,1,0:T(8,128)(2,1)} %phi_ref.1), calls=%async_computation.1 | async-start | bytes 1048576 | tf_op jit(solution)/shard_map/all_to_all | solution.py:237
  29.8 8.4 %shard_map.68 = f32[32,256]{1,0:T(8,128)S(1)} custom-call(bf16[256,32,1024]{2,1,0:T(8,128)(2,1)} %chol_hbm.7, bf16[1024,256]{1,0:T(8,128)(2,1)S(1)} %bitcast.36, bf16[32,32,256]{2,1,0:T(8,128)(2,1)S(1)} %copy-done.1), custom_call_target="tpu_custom_call" | custom-call | flops 4294967296 | bytes 16777216 | tf_op jit(solution)/shard_map/pallas_call | solution.py:139
  41.2 2.3 collective-permute-start.2
  45.7 3.6 %collective-permute-start.7 = (f32[16,256]{1,0:T(8,128)S(1)}, f32[16,256]{1,0:T(8,128)S(1)}, u32[]{:S(2)}, u32[]{:S(2)}) collective-permute-start(f32[16,256]{1,0:T(8,128)S(1)} %add_add_fusion.1), channel_id=1, source_target_pairs={{0,48},{16,0},{32,16},{48,32},{1,49},{17,1},{33,17},{49,33},{2,50}... | collective-permute-start | bytes 49160 | tf_op jit(solution)/shard_map/ppermute | solution.py:250
  49.3 2.3 collective-permute-start.6
  51.6 2.4 collective-permute-start.5
  54.0 2.9 %collective-permute-done.6 = f32[16,256]{1,0:T(8,128)S(1)} collective-permute-done((f32[16,256]{1,0:T(8,128)S(1)}, f32[16,256]{1,0:T(8,128)S(1)}, u32[]{:S(2)}, u32[]{:S(2)}) %collective-permute-start.6) | collective-permute-done | bytes 16416 | tf_op jit(solution)/shard_map/ppermute | solution.py:250
  58.8 8.8 %shard_map.69 = bf16[32,32,1024]{2,1,0:T(8,128)(2,1)} custom-call(bf16[32,256]{1,0:T(8,128)(2,1)S(1)} %fusion.mixed_ref, bf16[256,32,1024]{2,1,0:T(8,128)(2,1)} %chol_hbm.7), custom_call_target="tpu_custom_call" | custom-call | tf_op jit(solution)/shard_map/pallas_call | solution.py:222
  67.7 8.7 %all-to-all-start.2 = ((bf16[32,32,1024]{2,1,0:T(8,128)(2,1)}), bf16[32,32,1024]{2,1,0:T(8,128)(2,1)S(1)}, u32[]{:S(2)}, u32[]{:S(2)}) async-start(bf16[32,32,1024]{2,1,0:T(8,128)(2,1)} %shard_map.69), calls=%async_computation.2 | async-start | bytes 4194304 | tf_op jit(solution)/shard_map/all_to_all | solution.py:237
  76.4 8.6 %shard_map.70.rotated_ref = bf16[256,32,256]{2,1,0:T(8,128)(2,1)} custom-call(bf16[256,32,1024]{2,1,0:T(8,128)(2,1)} %chol_hbm.7, bf16[1024,256]{1,0:T(8,128)(2,1)S(1)} %bitcast.37), custom_call_target="tpu_custom_call" | custom-call | flops 4294967296 | bytes 16777216 | tf_op jit(solution)/shard_map/pallas_call | solution.py:182
  85.1 38.2 %all-to-all-done.2 = bf16[32,32,1024]{2,1,0:T(8,128)(2,1)S(1)} async-done(((bf16[32,32,1024]{2,1,0:T(8,128)(2,1)}), bf16[32,32,1024]{2,1,0:T(8,128)(2,1)S(1)}, u32[]{:S(2)}, u32[]{:S(2)}) %all-to-all-start.2) | async-done | bytes 2097184 | tf_op jit(solution)/shard_map/all_to_all | solution.py:237
  123.3 2.6 shard_map.71.walker_ref
  125.9 23.3 %all_to_all.36.phi_ref = bf16[32,32,256]{2,1,0:T(8,128)(2,1)S(1)} all-to-all(bf16[32,32,256]{2,1,0:T(8,128)(2,1)S(1)} %bitcast.41), channel_id=1, replica_groups=mesh['x'=4,'zh'=4,'c'=2,'y'=4,'zl'=2] {'x','zh','c'}, dimensions={0} | all-to-all | bytes 1048576 | tf_op jit(solution)/shard_map/all_to_all | solution.py:237
  149.2 1.9 shard_map.72
  151.1 2.5 collective-permute-start.9
  154.5 16.8 %all_to_all.37 = f32[16,16,256]{2,1,0:T(8,128)S(1)} all-to-all(f32[16,16,256]{2,1,0:T(8,128)S(1)} %broadcast_in_dim.5), channel_id=1, replica_groups=mesh['x'=4,'zh'=4,'c'=2,'y'=4,'zl'=2] {'x','zh'}, dimensions={0} | all-to-all | bytes 524288 | tf_op jit(solution)/shard_map/all_to_all | solution.py:237
  173.8 7.5 %shard_map.73 = bf16[32,32,1024]{2,1,0:T(8,128)(2,1)S(1)} custom-call(bf16[32,256]{1,0:T(8,128)(2,1)S(1)} %get-tuple-element.22.mixed_ref, bf16[256,32,1024]{2,1,0:T(8,128)(2,1)} %chol_hbm.7), custom_call_target="tpu_custom_call" | custom-call | tf_op jit(solution)/shard_map/pallas_call | solution.py:222
  181.3 56.1 %all_to_all.38 = bf16[32,32,1024]{2,1,0:T(8,128)(2,1)S(1)} all-to-all(bf16[32,32,1024]{2,1,0:T(8,128)(2,1)S(1)} %shard_map.73), channel_id=1, replica_groups=mesh['x'=4,'zh'=4,'c'=2,'y'=4,'zl'=2] {'x','zh','c'}, dimensions={0} | all-to-all | bytes 4194304 | tf_op jit(solution)/shard_map/all_to_all | solution.py:237
  237.5 3.4 %shard_map.74 = bf16[1024,256]{1,0:T(8,128)(2,1)} custom-call(bf16[1024,1024]{1,0:T(8,128)(2,1)S(1)} %bitcast.39, bf16[1024,256]{1,0:T(8,128)(2,1)S(1)} %shard_map.71.walker_ref), custom_call_target="tpu_custom_call" | custom-call | flops 2147483648 | bytes 4194304 | tf_op jit(solution)/shard_map/pallas_call | solution.py:301
  240.8 6.5 %all-to-all-start.6 = ((bf16[32,32,256]{2,1,0:T(8,128)(2,1)}), bf16[32,32,256]{2,1,0:T(8,128)(2,1)S(1)}, u32[]{:S(2)}, u32[]{:S(2)}) async-start(bf16[32,32,256]{2,1,0:T(8,128)(2,1)} %bitcast.15), calls=%async_computation.6 | async-start | bytes 1048576 | tf_op jit(solution)/shard_map/all_to_all | solution.py:237
  247.4 2.9 %collective-permute-start.14 = (f32[64]{0:T(128)S(1)}, f32[64]{0:T(128)S(1)}, u32[]{:S(2)}, u32[]{:S(2)}) collective-permute-start(f32[64]{0:T(128)S(1)} %pad_maximum_fusion), channel_id=1, source_target_pairs={{0,6},{2,0},{4,2},{6,4},{1,7},{3,1},{5,3},{7,5},{8,14},{10,8},{12,... | collective-permute-start | bytes 776 | tf_op jit(solution)/shard_map/ppermute | solution.py:250
  252.0 3.4 %collective-permute-done.13 = f32[64]{0:T(128)S(1)} collective-permute-done((f32[64]{0:T(128)S(1)}, f32[64]{0:T(128)S(1)}, u32[]{:S(2)}, u32[]{:S(2)}) %collective-permute-start.13) | collective-permute-done | bytes 288 | tf_op jit(solution)/shard_map/ppermute | solution.py:250
  257.7 5.5 %all-to-all-done.6 = bf16[32,32,256]{2,1,0:T(8,128)(2,1)S(1)} async-done(((bf16[32,32,256]{2,1,0:T(8,128)(2,1)}), bf16[32,32,256]{2,1,0:T(8,128)(2,1)S(1)}, u32[]{:S(2)}, u32[]{:S(2)}) %all-to-all-start.6) | async-done | bytes 524320 | tf_op jit(solution)/shard_map/all_to_all | solution.py:237
  (49 shorter events, 15.4 us)
Async XLA Ops:
  0.6 29.2 %copy-start.1 = (bf16[32,32,256]{2,1,0:T(8,128)(2,1)S(1)}, bf16[32,32,256]{2,1,0:T(8,128)(2,1)}, u32[]{:S(2)}) copy-start(bf16[32,32,256]{2,1,0:T(8,128)(2,1)} %phi_ref.1) | copy-start | bytes 1572868
  23.6 6.1 %collective-permute-start = (bf16[16,32,256]{2,1,0:T(8,128)(2,1)S(1)}, bf16[16,32,256]{2,1,0:T(8,128)(2,1)S(1)}, u32[]{:S(2)}, u32[]{:S(2)}) collective-permute-start(bf16[16,32,256]{2,1,0:T(8,128)(2,1)S(1)} %all_to_all.35), channel_id=1, source_target_pairs={{0,8},{8,0},{1,9},{9,1},{2,10},{10,2},{3,11},{11,3},{4,12},{12,4},... | collective-permute-start | bytes 786440 | tf_op jit(solution)/shard_map/ppermute | solution.py:241
  23.6 44.0 %all-to-all-start.1 = ((bf16[32,32,256]{2,1,0:T(8,128)(2,1)}), bf16[32,32,256]{2,1,0:T(8,128)(2,1)S(1)}, u32[]{:S(2)}, u32[]{:S(2)}) async-start(bf16[32,32,256]{2,1,0:T(8,128)(2,1)} %phi_ref.1), calls=%async_computation.1 | async-start | bytes 1048576 | tf_op jit(solution)/shard_map/all_to_all | solution.py:237
  29.8 29.0 %copy-start.2 = (f32[2,32,256]{2,1,0:T(8,128)S(1)}, f32[2,32,256]{2,1,0:T(8,128)}, u32[]{:S(2)}) copy-start(f32[2,32,256]{2,1,0:T(8,128)} %param.8) | copy-start | bytes 196612
  38.2 1.3 collective-permute-start.1
  39.5 5.1 %collective-permute-start.4 = (f32[16,256]{1,0:T(8,128)S(1)}, f32[16,256]{1,0:T(8,128)S(1)}, u32[]{:S(2)}, u32[]{:S(2)}) collective-permute-start(f32[16,256]{1,0:T(8,128)S(1)} %bitcast_add_fusion.1), channel_id=1, source_target_pairs={{0,192},{64,0},{128,64},{192,128},{1,193},{65,1},{129,65},{193,129... | collective-permute-start | bytes 49160 | tf_op jit(solution)/shard_map/ppermute | solution.py:250
  40.3 5.4 %collective-permute-start.3 = (f32[16,256]{1,0:T(8,128)S(1)}, f32[16,256]{1,0:T(8,128)S(1)}, u32[]{:S(2)}, u32[]{:S(2)}) collective-permute-start(f32[16,256]{1,0:T(8,128)S(1)} %bitcast_add_fusion.1), channel_id=1, source_target_pairs={{0,128},{64,192},{128,0},{192,64},{1,129},{65,193},{129,1},{193,65... | collective-permute-start | bytes 49160 | tf_op jit(solution)/shard_map/ppermute | solution.py:250
  41.2 4.5 %collective-permute-start.2 = (f32[16,256]{1,0:T(8,128)S(1)}, f32[16,256]{1,0:T(8,128)S(1)}, u32[]{:S(2)}, u32[]{:S(2)}) collective-permute-start(f32[16,256]{1,0:T(8,128)S(1)} %bitcast_add_fusion.1), channel_id=1, source_target_pairs={{0,64},{64,128},{128,192},{192,0},{1,65},{65,129},{129,193},{193,1... | collective-permute-start | bytes 49160 | tf_op jit(solution)/shard_map/ppermute | solution.py:250
  45.7 8.3 %collective-permute-start.7 = (f32[16,256]{1,0:T(8,128)S(1)}, f32[16,256]{1,0:T(8,128)S(1)}, u32[]{:S(2)}, u32[]{:S(2)}) collective-permute-start(f32[16,256]{1,0:T(8,128)S(1)} %add_add_fusion.1), channel_id=1, source_target_pairs={{0,48},{16,0},{32,16},{48,32},{1,49},{17,1},{33,17},{49,33},{2,50}... | collective-permute-start | bytes 49160 | tf_op jit(solution)/shard_map/ppermute | solution.py:250
  49.3 7.6 %collective-permute-start.6 = (f32[16,256]{1,0:T(8,128)S(1)}, f32[16,256]{1,0:T(8,128)S(1)}, u32[]{:S(2)}, u32[]{:S(2)}) collective-permute-start(f32[16,256]{1,0:T(8,128)S(1)} %add_add_fusion.1), channel_id=1, source_target_pairs={{0,32},{16,48},{32,0},{48,16},{1,33},{17,49},{33,1},{49,17},{2,34}... | collective-permute-start | bytes 49160 | tf_op jit(solution)/shard_map/ppermute | solution.py:250
  51.6 5.9 %collective-permute-start.5 = (f32[16,256]{1,0:T(8,128)S(1)}, f32[16,256]{1,0:T(8,128)S(1)}, u32[]{:S(2)}, u32[]{:S(2)}) collective-permute-start(f32[16,256]{1,0:T(8,128)S(1)} %add_add_fusion.1), channel_id=1, source_target_pairs={{0,16},{16,32},{32,48},{48,0},{1,17},{17,33},{33,49},{49,1},{2,18}... | collective-permute-start | bytes 49160 | tf_op jit(solution)/shard_map/ppermute | solution.py:250
  57.5 1.3 collective-permute-start.8
  67.7 55.6 %all-to-all-start.2 = ((bf16[32,32,1024]{2,1,0:T(8,128)(2,1)}), bf16[32,32,1024]{2,1,0:T(8,128)(2,1)S(1)}, u32[]{:S(2)}, u32[]{:S(2)}) async-start(bf16[32,32,1024]{2,1,0:T(8,128)(2,1)} %shard_map.69), calls=%async_computation.2 | async-start | bytes 4194304 | tf_op jit(solution)/shard_map/all_to_all | solution.py:237
  123.3 25.9 %copy-start = (bf16[256,32,256]{2,1,0:T(8,128)(2,1)S(1)}, bf16[256,32,256]{2,1,0:T(8,128)(2,1)}, u32[]{:S(2)}) copy-start(bf16[256,32,256]{2,1,0:T(8,128)(2,1)} %shard_map.70.rotated_ref) | copy-start | bytes 12582916
  149.2 23.5 %copy-start.3 = (f32[32]{0:T(128)S(1)}, f32[32]{0:T(128)}, u32[]{:S(2)}) copy-start(f32[32]{0:T(128)} %param.9) | copy-start | bytes 388
  151.1 3.3 %collective-permute-start.9 = (f32[16,256]{1,0:T(8,128)S(1)}, f32[16,256]{1,0:T(8,128)S(1)}, u32[]{:S(2)}, u32[]{:S(2)}) collective-permute-start(f32[16,256]{1,0:T(8,128)S(1)} %dynamic-slice_bitcast_fusion), channel_id=1, source_target_pairs={{0,8},{8,0},{1,9},{9,1},{2,10},{10,2},{3,11},{11,3},{4,12},{12,4},... | collective-permute-start | bytes 49160 | tf_op jit(solution)/shard_map/ppermute | solution.py:241
  171.3 1.3 collective-permute-start.10
  172.7 8.6 %collective-permute-start.11 = (f32[32]{0:T(128)S(1)}, f32[32]{0:T(128)S(1)}, u32[]{:S(2)}, u32[]{:S(2)}) collective-permute-start(f32[32]{0:T(128)S(1)} %add_add_fusion.2), channel_id=1, source_target_pairs={{0,1},{1,0},{2,3},{3,2},{4,5},{5,4},{6,7},{7,6},{8,9},{9,8},{10,11... | collective-permute-start | bytes 392 | tf_op jit(solution)/shard_map/ppermute | solution.py:241
  240.8 22.3 %all-to-all-start.6 = ((bf16[32,32,256]{2,1,0:T(8,128)(2,1)}), bf16[32,32,256]{2,1,0:T(8,128)(2,1)S(1)}, u32[]{:S(2)}, u32[]{:S(2)}) async-start(bf16[32,32,256]{2,1,0:T(8,128)(2,1)} %bitcast.15), calls=%async_computation.6 | async-start | bytes 1048576 | tf_op jit(solution)/shard_map/all_to_all | solution.py:237
  247.4 4.5 %collective-permute-start.14 = (f32[64]{0:T(128)S(1)}, f32[64]{0:T(128)S(1)}, u32[]{:S(2)}, u32[]{:S(2)}) collective-permute-start(f32[64]{0:T(128)S(1)} %pad_maximum_fusion), channel_id=1, source_target_pairs={{0,6},{2,0},{4,2},{6,4},{1,7},{3,1},{5,3},{7,5},{8,14},{10,8},{12,... | collective-permute-start | bytes 776 | tf_op jit(solution)/shard_map/ppermute | solution.py:250
  250.4 5.0 %collective-permute-start.13 = (f32[64]{0:T(128)S(1)}, f32[64]{0:T(128)S(1)}, u32[]{:S(2)}, u32[]{:S(2)}) collective-permute-start(f32[64]{0:T(128)S(1)} %pad_maximum_fusion), channel_id=1, source_target_pairs={{0,4},{2,6},{4,0},{6,2},{1,5},{3,7},{5,1},{7,3},{8,12},{10,14},{12... | collective-permute-start | bytes 776 | tf_op jit(solution)/shard_map/ppermute | solution.py:250
  251.0 4.8 %collective-permute-start.12 = (f32[64]{0:T(128)S(1)}, f32[64]{0:T(128)S(1)}, u32[]{:S(2)}, u32[]{:S(2)}) collective-permute-start(f32[64]{0:T(128)S(1)} %pad_maximum_fusion), channel_id=1, source_target_pairs={{0,2},{2,4},{4,6},{6,0},{1,3},{3,5},{5,7},{7,1},{8,10},{10,12},{12... | collective-permute-start | bytes 776 | tf_op jit(solution)/shard_map/ppermute | solution.py:250

commit v4 on v3

--- a/solution.py
+++ b/solution.py
@@ -288,7 +288,7 @@
         held = walker_ref if degree == 1 else term_ref.at[degree % 2]
         for low in range(0, orbitals, count):
             at = slice(low, low + count)
-            next_term = dot(potential_ref[at, :], held[...]) / degree
+            next_term = dot(potential_ref[at, :], held[...]) * (1.0 / degree)
             before = walker_ref[at, :].astype(jnp.float32) if degree == 1 else summed_ref[at, :]
             if degree < 4:
                 summed_ref[at, :] = before + next_term

time: 268 us -> 268 us (level)
  no operation moved by 1% of the time
where the time goes in v4:
time: 268 us; the launch traced here: 264 us
  blocking collectives  118 us (44%)
  waiting for transfers between devices  57.5 us (21%)
  starting transfers between devices  42.2 us (16%)
  Pallas kernels  41.1 us (15%)
    all_to_all x4, blocking collectives, exchange(): return lax.all_to_all(value, axis, split_axis=0, concat_axis=0, tiled=True)  118 us
    all_to_all x3, waiting for transfers between devices, exchange(): return lax.all_to_all(value, axis, split_axis=0, concat_axis=0, tiled=True)  43.8 us
    all_to_all x3, starting transfers between devices, exchange(): return lax.all_to_all(value, axis, split_axis=0, concat_axis=0, tiled=True)  21.3 us
    ppermute x9, starting transfers between devices, turn(): return lax.ppermute(value, axis, [(i, (i + shift) % 4) for i in range(4)])  16.8 us
    pallas_call x2, Pallas kernels, potential(): pl.pallas_call(potential_kernel, in_specs=[WHOLE, IN_HBM], out_specs=WHOL...  16.3 us
    ppermute x9, waiting for transfers between devices, turn(): return lax.ppermute(value, axis, [(i, (i + shift) % 4) for i in range(4)])  9.51 us
    pallas_call x1, Pallas kernels, rotate(): pl.pallas_call(rotate_kernel, in_specs=[IN_HBM, WHOLE], out_specs=IN_HBM,...  8.62 us
    pallas_call x1, Pallas kernels, first_bias(): pl.pallas_call(first_bias_kernel, in_specs=[IN_HBM, WHOLE, WHOLE], out_sp...  8.38 us
  transfers between devices with their start and end apart: 18, of which 12 were waited for; matrix products, arithmetic and copies ran while one was open for 1% of the time, Pallas kernels for 13%

profile of v4, /device:TPU:6, one launch (start us, length us, event | category | flops | bytes accessed | tf_op | source)
XLA Modules:
  0.0 264.0 jit_solution(7268912885201118670)
XLA Ops:
  1.4 22.2 %all_to_all.35 = bf16[16,32,256]{2,1,0:T(8,128)(2,1)S(1)} all-to-all(bf16[16,32,256]{2,1,0:T(8,128)(2,1)S(1)} %broadcast_in_dim.4), channel_id=1, replica_groups=mesh['x'=4,'zh'=4,'c'=2,'y'=4,'zl'=2] {'x','zh'}, dimensions={0} | all-to-all | bytes 524288 | tf_op jit(solution)/shard_map/all_to_all | solution.py:237
  23.6 6.1 %all-to-all-start.1 = ((bf16[32,32,256]{2,1,0:T(8,128)(2,1)}), bf16[32,32,256]{2,1,0:T(8,128)(2,1)S(1)}, u32[]{:S(2)}, u32[]{:S(2)}) async-start(bf16[32,32,256]{2,1,0:T(8,128)(2,1)} %phi_ref.1), calls=%async_computation.1 | async-start | bytes 1048576 | tf_op jit(solution)/shard_map/all_to_all | solution.py:237
  29.8 8.4 %shard_map.68 = f32[32,256]{1,0:T(8,128)S(1)} custom-call(bf16[256,32,1024]{2,1,0:T(8,128)(2,1)} %chol_hbm.7, bf16[1024,256]{1,0:T(8,128)(2,1)S(1)} %bitcast.36, bf16[32,32,256]{2,1,0:T(8,128)(2,1)S(1)} %copy-done.1), custom_call_target="tpu_custom_call" | custom-call | flops 4294967296 | bytes 16777216 | tf_op jit(solution)/shard_map/pallas_call | solution.py:139
  41.2 2.3 collective-permute-start.2
  45.7 3.6 %collective-permute-start.7 = (f32[16,256]{1,0:T(8,128)S(1)}, f32[16,256]{1,0:T(8,128)S(1)}, u32[]{:S(2)}, u32[]{:S(2)}) collective-permute-start(f32[16,256]{1,0:T(8,128)S(1)} %add_add_fusion.1), channel_id=1, source_target_pairs={{0,48},{16,0},{32,16},{48,32},{1,49},{17,1},{33,17},{49,33},{2,50}... | collective-permute-start | bytes 49160 | tf_op jit(solution)/shard_map/ppermute | solution.py:250
  49.3 2.3 collective-permute-start.6
  51.6 2.4 collective-permute-start.5
  54.0 2.9 %collective-permute-done.6 = f32[16,256]{1,0:T(8,128)S(1)} collective-permute-done((f32[16,256]{1,0:T(8,128)S(1)}, f32[16,256]{1,0:T(8,128)S(1)}, u32[]{:S(2)}, u32[]{:S(2)}) %collective-permute-start.6) | collective-permute-done | bytes 16416 | tf_op jit(solution)/shard_map/ppermute | solution.py:250
  58.8 8.8 %shard_map.69 = bf16[32,32,1024]{2,1,0:T(8,128)(2,1)} custom-call(bf16[32,256]{1,0:T(8,128)(2,1)S(1)} %fusion.mixed_ref, bf16[256,32,1024]{2,1,0:T(8,128)(2,1)} %chol_hbm.7), custom_call_target="tpu_custom_call" | custom-call | tf_op jit(solution)/shard_map/pallas_call | solution.py:222
  67.7 8.7 %all-to-all-start.2 = ((bf16[32,32,1024]{2,1,0:T(8,128)(2,1)}), bf16[32,32,1024]{2,1,0:T(8,128)(2,1)S(1)}, u32[]{:S(2)}, u32[]{:S(2)}) async-start(bf16[32,32,1024]{2,1,0:T(8,128)(2,1)} %shard_map.69), calls=%async_computation.2 | async-start | bytes 4194304 | tf_op jit(solution)/shard_map/all_to_all | solution.py:237
  76.4 8.6 %shard_map.70.rotated_ref = bf16[256,32,256]{2,1,0:T(8,128)(2,1)} custom-call(bf16[256,32,1024]{2,1,0:T(8,128)(2,1)} %chol_hbm.7, bf16[1024,256]{1,0:T(8,128)(2,1)S(1)} %bitcast.37), custom_call_target="tpu_custom_call" | custom-call | flops 4294967296 | bytes 16777216 | tf_op jit(solution)/shard_map/pallas_call | solution.py:182
  85.1 38.2 %all-to-all-done.2 = bf16[32,32,1024]{2,1,0:T(8,128)(2,1)S(1)} async-done(((bf16[32,32,1024]{2,1,0:T(8,128)(2,1)}), bf16[32,32,1024]{2,1,0:T(8,128)(2,1)S(1)}, u32[]{:S(2)}, u32[]{:S(2)}) %all-to-all-start.2) | async-done | bytes 2097184 | tf_op jit(solution)/shard_map/all_to_all | solution.py:237
  123.3 2.6 shard_map.71.walker_ref
  125.9 23.3 %all_to_all.36.phi_ref = bf16[32,32,256]{2,1,0:T(8,128)(2,1)S(1)} all-to-all(bf16[32,32,256]{2,1,0:T(8,128)(2,1)S(1)} %bitcast.41), channel_id=1, replica_groups=mesh['x'=4,'zh'=4,'c'=2,'y'=4,'zl'=2] {'x','zh','c'}, dimensions={0} | all-to-all | bytes 1048576 | tf_op jit(solution)/shard_map/all_to_all | solution.py:237
  149.2 1.9 shard_map.72
  151.1 2.5 collective-permute-start.9
  154.5 16.8 %all_to_all.37 = f32[16,16,256]{2,1,0:T(8,128)S(1)} all-to-all(f32[16,16,256]{2,1,0:T(8,128)S(1)} %broadcast_in_dim.5), channel_id=1, replica_groups=mesh['x'=4,'zh'=4,'c'=2,'y'=4,'zl'=2] {'x','zh'}, dimensions={0} | all-to-all | bytes 524288 | tf_op jit(solution)/shard_map/all_to_all | solution.py:237
  173.8 7.5 %shard_map.73 = bf16[32,32,1024]{2,1,0:T(8,128)(2,1)S(1)} custom-call(bf16[32,256]{1,0:T(8,128)(2,1)S(1)} %get-tuple-element.22.mixed_ref, bf16[256,32,1024]{2,1,0:T(8,128)(2,1)} %chol_hbm.7), custom_call_target="tpu_custom_call" | custom-call | tf_op jit(solution)/shard_map/pallas_call | solution.py:222
  181.3 56.1 %all_to_all.38 = bf16[32,32,1024]{2,1,0:T(8,128)(2,1)S(1)} all-to-all(bf16[32,32,1024]{2,1,0:T(8,128)(2,1)S(1)} %shard_map.73), channel_id=1, replica_groups=mesh['x'=4,'zh'=4,'c'=2,'y'=4,'zl'=2] {'x','zh','c'}, dimensions={0} | all-to-all | bytes 4194304 | tf_op jit(solution)/shard_map/all_to_all | solution.py:237
  237.5 3.4 %shard_map.74 = bf16[1024,256]{1,0:T(8,128)(2,1)} custom-call(bf16[1024,1024]{1,0:T(8,128)(2,1)S(1)} %bitcast.39, bf16[1024,256]{1,0:T(8,128)(2,1)S(1)} %shard_map.71.walker_ref), custom_call_target="tpu_custom_call" | custom-call | flops 2147483648 | bytes 4194304 | tf_op jit(solution)/shard_map/pallas_call | solution.py:301
  240.8 6.5 %all-to-all-start.6 = ((bf16[32,32,256]{2,1,0:T(8,128)(2,1)}), bf16[32,32,256]{2,1,0:T(8,128)(2,1)S(1)}, u32[]{:S(2)}, u32[]{:S(2)}) async-start(bf16[32,32,256]{2,1,0:T(8,128)(2,1)} %bitcast.15), calls=%async_computation.6 | async-start | bytes 1048576 | tf_op jit(solution)/shard_map/all_to_all | solution.py:237
  247.4 2.9 %collective-permute-start.14 = (f32[64]{0:T(128)S(1)}, f32[64]{0:T(128)S(1)}, u32[]{:S(2)}, u32[]{:S(2)}) collective-permute-start(f32[64]{0:T(128)S(1)} %pad_maximum_fusion), channel_id=1, source_target_pairs={{0,6},{2,0},{4,2},{6,4},{1,7},{3,1},{5,3},{7,5},{8,14},{10,8},{12,... | collective-permute-start | bytes 776 | tf_op jit(solution)/shard_map/ppermute | solution.py:250
  252.0 3.4 %collective-permute-done.13 = f32[64]{0:T(128)S(1)} collective-permute-done((f32[64]{0:T(128)S(1)}, f32[64]{0:T(128)S(1)}, u32[]{:S(2)}, u32[]{:S(2)}) %collective-permute-start.13) | collective-permute-done | bytes 288 | tf_op jit(solution)/shard_map/ppermute | solution.py:250
  257.7 5.5 %all-to-all-done.6 = bf16[32,32,256]{2,1,0:T(8,128)(2,1)S(1)} async-done(((bf16[32,32,256]{2,1,0:T(8,128)(2,1)}), bf16[32,32,256]{2,1,0:T(8,128)(2,1)S(1)}, u32[]{:S(2)}, u32[]{:S(2)}) %all-to-all-start.6) | async-done | bytes 524320 | tf_op jit(solution)/shard_map/all_to_all | solution.py:237
  (49 shorter events, 15.4 us)
Async XLA Ops:
  0.6 29.2 %copy-start.1 = (bf16[32,32,256]{2,1,0:T(8,128)(2,1)S(1)}, bf16[32,32,256]{2,1,0:T(8,128)(2,1)}, u32[]{:S(2)}) copy-start(bf16[32,32,256]{2,1,0:T(8,128)(2,1)} %phi_ref.1) | copy-start | bytes 1572868
  23.6 6.1 %collective-permute-start = (bf16[16,32,256]{2,1,0:T(8,128)(2,1)S(1)}, bf16[16,32,256]{2,1,0:T(8,128)(2,1)S(1)}, u32[]{:S(2)}, u32[]{:S(2)}) collective-permute-start(bf16[16,32,256]{2,1,0:T(8,128)(2,1)S(1)} %all_to_all.35), channel_id=1, source_target_pairs={{0,8},{8,0},{1,9},{9,1},{2,10},{10,2},{3,11},{11,3},{4,12},{12,4},... | collective-permute-start | bytes 786440 | tf_op jit(solution)/shard_map/ppermute | solution.py:241
  23.6 44.0 %all-to-all-start.1 = ((bf16[32,32,256]{2,1,0:T(8,128)(2,1)}), bf16[32,32,256]{2,1,0:T(8,128)(2,1)S(1)}, u32[]{:S(2)}, u32[]{:S(2)}) async-start(bf16[32,32,256]{2,1,0:T(8,128)(2,1)} %phi_ref.1), calls=%async_computation.1 | async-start | bytes 1048576 | tf_op jit(solution)/shard_map/all_to_all | solution.py:237
  29.8 29.0 %copy-start.2 = (f32[2,32,256]{2,1,0:T(8,128)S(1)}, f32[2,32,256]{2,1,0:T(8,128)}, u32[]{:S(2)}) copy-start(f32[2,32,256]{2,1,0:T(8,128)} %param.8) | copy-start | bytes 196612
  38.2 1.3 collective-permute-start.1
  39.5 5.1 %collective-permute-start.4 = (f32[16,256]{1,0:T(8,128)S(1)}, f32[16,256]{1,0:T(8,128)S(1)}, u32[]{:S(2)}, u32[]{:S(2)}) collective-permute-start(f32[16,256]{1,0:T(8,128)S(1)} %bitcast_add_fusion.1), channel_id=1, source_target_pairs={{0,192},{64,0},{128,64},{192,128},{1,193},{65,1},{129,65},{193,129... | collective-permute-start | bytes 49160 | tf_op jit(solution)/shard_map/ppermute | solution.py:250
  40.3 5.4 %collective-permute-start.3 = (f32[16,256]{1,0:T(8,128)S(1)}, f32[16,256]{1,0:T(8,128)S(1)}, u32[]{:S(2)}, u32[]{:S(2)}) collective-permute-start(f32[16,256]{1,0:T(8,128)S(1)} %bitcast_add_fusion.1), channel_id=1, source_target_pairs={{0,128},{64,192},{128,0},{192,64},{1,129},{65,193},{129,1},{193,65... | collective-permute-start | bytes 49160 | tf_op jit(solution)/shard_map/ppermute | solution.py:250
  41.2 4.5 %collective-permute-start.2 = (f32[16,256]{1,0:T(8,128)S(1)}, f32[16,256]{1,0:T(8,128)S(1)}, u32[]{:S(2)}, u32[]{:S(2)}) collective-permute-start(f32[16,256]{1,0:T(8,128)S(1)} %bitcast_add_fusion.1), channel_id=1, source_target_pairs={{0,64},{64,128},{128,192},{192,0},{1,65},{65,129},{129,193},{193,1... | collective-permute-start | bytes 49160 | tf_op jit(solution)/shard_map/ppermute | solution.py:250
  45.7 8.3 %collective-permute-start.7 = (f32[16,256]{1,0:T(8,128)S(1)}, f32[16,256]{1,0:T(8,128)S(1)}, u32[]{:S(2)}, u32[]{:S(2)}) collective-permute-start(f32[16,256]{1,0:T(8,128)S(1)} %add_add_fusion.1), channel_id=1, source_target_pairs={{0,48},{16,0},{32,16},{48,32},{1,49},{17,1},{33,17},{49,33},{2,50}... | collective-permute-start | bytes 49160 | tf_op jit(solution)/shard_map/ppermute | solution.py:250
  49.3 7.6 %collective-permute-start.6 = (f32[16,256]{1,0:T(8,128)S(1)}, f32[16,256]{1,0:T(8,128)S(1)}, u32[]{:S(2)}, u32[]{:S(2)}) collective-permute-start(f32[16,256]{1,0:T(8,128)S(1)} %add_add_fusion.1), channel_id=1, source_target_pairs={{0,32},{16,48},{32,0},{48,16},{1,33},{17,49},{33,1},{49,17},{2,34}... | collective-permute-start | bytes 49160 | tf_op jit(solution)/shard_map/ppermute | solution.py:250
  51.6 5.9 %collective-permute-start.5 = (f32[16,256]{1,0:T(8,128)S(1)}, f32[16,256]{1,0:T(8,128)S(1)}, u32[]{:S(2)}, u32[]{:S(2)}) collective-permute-start(f32[16,256]{1,0:T(8,128)S(1)} %add_add_fusion.1), channel_id=1, source_target_pairs={{0,16},{16,32},{32,48},{48,0},{1,17},{17,33},{33,49},{49,1},{2,18}... | collective-permute-start | bytes 49160 | tf_op jit(solution)/shard_map/ppermute | solution.py:250
  57.5 1.3 collective-permute-start.8
  67.7 55.6 %all-to-all-start.2 = ((bf16[32,32,1024]{2,1,0:T(8,128)(2,1)}), bf16[32,32,1024]{2,1,0:T(8,128)(2,1)S(1)}, u32[]{:S(2)}, u32[]{:S(2)}) async-start(bf16[32,32,1024]{2,1,0:T(8,128)(2,1)} %shard_map.69), calls=%async_computation.2 | async-start | bytes 4194304 | tf_op jit(solution)/shard_map/all_to_all | solution.py:237
  123.3 25.9 %copy-start = (bf16[256,32,256]{2,1,0:T(8,128)(2,1)S(1)}, bf16[256,32,256]{2,1,0:T(8,128)(2,1)}, u32[]{:S(2)}) copy-start(bf16[256,32,256]{2,1,0:T(8,128)(2,1)} %shard_map.70.rotated_ref) | copy-start | bytes 12582916
  149.2 23.5 %copy-start.3 = (f32[32]{0:T(128)S(1)}, f32[32]{0:T(128)}, u32[]{:S(2)}) copy-start(f32[32]{0:T(128)} %param.9) | copy-start | bytes 388
  151.1 3.3 %collective-permute-start.9 = (f32[16,256]{1,0:T(8,128)S(1)}, f32[16,256]{1,0:T(8,128)S(1)}, u32[]{:S(2)}, u32[]{:S(2)}) collective-permute-start(f32[16,256]{1,0:T(8,128)S(1)} %dynamic-slice_bitcast_fusion), channel_id=1, source_target_pairs={{0,8},{8,0},{1,9},{9,1},{2,10},{10,2},{3,11},{11,3},{4,12},{12,4},... | collective-permute-start | bytes 49160 | tf_op jit(solution)/shard_map/ppermute | solution.py:241
  171.3 1.3 collective-permute-start.10
  172.7 8.6 %collective-permute-start.11 = (f32[32]{0:T(128)S(1)}, f32[32]{0:T(128)S(1)}, u32[]{:S(2)}, u32[]{:S(2)}) collective-permute-start(f32[32]{0:T(128)S(1)} %add_add_fusion.2), channel_id=1, source_target_pairs={{0,1},{1,0},{2,3},{3,2},{4,5},{5,4},{6,7},{7,6},{8,9},{9,8},{10,11... | collective-permute-start | bytes 392 | tf_op jit(solution)/shard_map/ppermute | solution.py:241
  240.8 22.3 %all-to-all-start.6 = ((bf16[32,32,256]{2,1,0:T(8,128)(2,1)}), bf16[32,32,256]{2,1,0:T(8,128)(2,1)S(1)}, u32[]{:S(2)}, u32[]{:S(2)}) async-start(bf16[32,32,256]{2,1,0:T(8,128)(2,1)} %bitcast.15), calls=%async_computation.6 | async-start | bytes 1048576 | tf_op jit(solution)/shard_map/all_to_all | solution.py:237
  247.4 4.5 %collective-permute-start.14 = (f32[64]{0:T(128)S(1)}, f32[64]{0:T(128)S(1)}, u32[]{:S(2)}, u32[]{:S(2)}) collective-permute-start(f32[64]{0:T(128)S(1)} %pad_maximum_fusion), channel_id=1, source_target_pairs={{0,6},{2,0},{4,2},{6,4},{1,7},{3,1},{5,3},{7,5},{8,14},{10,8},{12,... | collective-permute-start | bytes 776 | tf_op jit(solution)/shard_map/ppermute | solution.py:250
  250.4 5.0 %collective-permute-start.13 = (f32[64]{0:T(128)S(1)}, f32[64]{0:T(128)S(1)}, u32[]{:S(2)}, u32[]{:S(2)}) collective-permute-start(f32[64]{0:T(128)S(1)} %pad_maximum_fusion), channel_id=1, source_target_pairs={{0,4},{2,6},{4,0},{6,2},{1,5},{3,7},{5,1},{7,3},{8,12},{10,14},{12... | collective-permute-start | bytes 776 | tf_op jit(solution)/shard_map/ppermute | solution.py:250
  251.0 4.8 %collective-permute-start.12 = (f32[64]{0:T(128)S(1)}, f32[64]{0:T(128)S(1)}, u32[]{:S(2)}, u32[]{:S(2)}) collective-permute-start(f32[64]{0:T(128)S(1)} %pad_maximum_fusion), channel_id=1, source_target_pairs={{0,2},{2,4},{4,6},{6,0},{1,3},{3,5},{5,7},{7,1},{8,10},{10,12},{12... | collective-permute-start | bytes 776 | tf_op jit(solution)/shard_map/ppermute | solution.py:250
